TPU v7x, 32 devices: a whole 2x2x4 slice. The times are simulated.
32 devices in a mesh: dp: 4 (over y, core), mp: 8 (over z, x).
Axes of the slice: x: 2, y: 2, z: 4, core: 2. Of those that a mesh axis runs over, the one named last changes fastest.
Arguments:
- tokens: bfloat16 [128, 3072], P(('dp', 'mp')), may hold values from -6 to 6
- cotangent: bfloat16 [128, 3072], P(('dp', 'mp')), may hold values from -6 to 6
- up_weight: bfloat16 [3072, 12288], P(None, 'mp'), may hold values from -0.109375 to 0.109375
- down_weight: bfloat16 [12288, 3072], P('mp'), may hold values from -0.0546875 to 0.0546875
Outputs:
- mixed_out: bfloat16 [128, 3072], P(('dp', 'mp'))
- token_gradient: bfloat16 [128, 3072], P(('dp', 'mp'))
- up_grad: bfloat16 [3072, 12288], P('dp', 'mp')
- down_grad: bfloat16 [12288, 3072], P('mp', 'dp')
All inputs are finite; a program needn't handle non-finite values.
Results may differ from a plain program's by a relative error of at most 0.02.
Values may be sent and summed in bfloat16 or wider, within the bound.
A program may use at most 128 MiB of HBM per device.

v0:
```python
import jax
import jax.numpy as jnp
from jax import lax
from jax.sharding import PartitionSpec as P

root_half = 0.7071067811865476
density_scale = 0.3989422804014327


def standardise_rows(tokens):
    values = tokens.astype(jnp.float32)
    row_mean = jnp.mean(values, axis=1, keepdims=True)
    centred = values - row_mean
    variance = jnp.mean(centred * centred, axis=1, keepdims=True)
    reciprocal_spread = lax.rsqrt(variance + 1e-06)
    return (centred * reciprocal_spread, reciprocal_spread)


def gelu_parts(pre_act):
    cumulative = 0.5 * (1.0 + lax.erf(pre_act * root_half))
    density = jnp.exp(-0.5 * pre_act * pre_act) * density_scale
    return (pre_act * cumulative, cumulative + pre_act * density)


def shard_sum(left_rows, right_rows, n_shards, shard_len):
    left_blocks = left_rows.reshape(n_shards, shard_len, left_rows.shape[1])
    right_blocks = right_rows.reshape(n_shards, shard_len, right_rows.shape[1])
    per_shard = jnp.einsum(
        "nta,ntb->nab", left_blocks, right_blocks, preferred_element_type=jnp.float32
    )
    per_shard = lax.optimization_barrier(per_shard.astype(jnp.bfloat16)).astype(jnp.float32)
    return jnp.sum(per_shard, axis=0)


def body(tokens, cotangent, up_weight, down_weight):
    centred_scaled_input, reciprocal_spread = standardise_rows(tokens)
    standardised_input = centred_scaled_input.astype(jnp.bfloat16)
    normed_all, cot_all = (
        lax.all_gather(standardised_input, "mp", axis=0, tiled=True),
        lax.all_gather(cotangent, "mp", axis=0, tiled=True),
    )
    pre_act = jnp.dot(normed_all, up_weight, preferred_element_type=jnp.float32)
    gelu_value, gelu_slope = gelu_parts(pre_act)
    hidden = gelu_value.astype(jnp.bfloat16)
    block_out = lax.psum_scatter(
        jnp.dot(hidden, down_weight, preferred_element_type=jnp.float32).astype(jnp.bfloat16),
        "mp",
        scatter_dimension=0,
        tiled=True,
    ).astype(jnp.float32)
    mixed_out = (tokens.astype(jnp.float32) + block_out).astype(jnp.bfloat16)
    hidden_grad = lax.dot_general(
        cot_all, down_weight, (((1,), (1,)), ((), ())), preferred_element_type=jnp.float32
    )
    act_grad = (hidden_grad * gelu_slope).astype(jnp.bfloat16)
    standardised_gradient = lax.psum_scatter(
        lax.dot_general(
            act_grad, up_weight, (((1,), (1,)), ((), ())), preferred_element_type=jnp.float32
        ).astype(jnp.bfloat16),
        "mp",
        scatter_dimension=0,
        tiled=True,
    ).astype(jnp.float32)
    gradient_average = jnp.mean(standardised_gradient, axis=1, keepdims=True)
    projection_average = jnp.mean(
        standardised_gradient * centred_scaled_input, axis=1, keepdims=True
    )
    token_gradient = cotangent.astype(jnp.float32) + reciprocal_spread * (
        standardised_gradient - gradient_average - centred_scaled_input * projection_average
    )
    token_gradient = token_gradient.astype(jnp.bfloat16)
    n_shards = lax.axis_size("dp")
    shard_len = normed_all.shape[0]
    normed_cols, cot_cols = (
        lax.all_to_all(normed_all, "dp", split_axis=1, concat_axis=0, tiled=True),
        lax.all_to_all(cot_all, "dp", split_axis=1, concat_axis=0, tiled=True),
    )
    hidden_dp, act_dp = (
        lax.all_gather(hidden, "dp", axis=0, tiled=True),
        lax.all_gather(act_grad, "dp", axis=0, tiled=True),
    )
    down_grad = shard_sum(hidden_dp, cot_cols, n_shards, shard_len)
    up_grad = shard_sum(normed_cols, act_dp, n_shards, shard_len)
    return (mixed_out, token_gradient, up_grad.astype(jnp.bfloat16), down_grad.astype(jnp.bfloat16))


def solution(mesh):
    return jax.shard_map(
        body,
        mesh=mesh,
        in_specs=(P(("dp", "mp"), None), P(("dp", "mp"), None), P(None, "mp"), P("mp", None)),
        out_specs=(P(("dp", "mp"), None), P(("dp", "mp"), None), P("dp", "mp"), P("mp", "dp")),
        check_vma=False,
    )
```

profile of v0, /device:TPU:0, one launch (start us, length us, event | category | flops | bytes accessed | tf_op | source)
XLA Modules:
  0.0 178.1 jit_solution(18427177174733176442)
XLA Ops:
  7.2 0.9 convert_reduce_fusion.1
  8.0 0.9 fusion.15
  9.0 0.8 fusion.18
  9.8 32.4 %all-gather = bf16[8,4,3072]{2,1,0:T(4,128)(2,1)S(1)} all-gather(bf16[1,4,3072]{2,1,0:T(4,128)(2,1)S(1)} %fusion.18), channel_id=1, replica_groups=mesh['dp'=4,'mp'=8] {'mp'}, dimensions={0}, use_global_device_ids=true | all-gather | bytes 221184 | tf_op jit(solution)/shard_map/all_gather | solution.py:39
  42.3 0.7 copy.12
  43.0 3.4 %all-to-all-start = ((bf16[32,4,768]{2,0,1:T(8,128)(2,1)}), bf16[32,4,768]{2,0,1:T(8,128)(2,1)S(1)}, u32[]{:S(2)}, u32[]{:S(2)}) async-start(bf16[32,4,768]{2,0,1:T(8,128)(2,1)} %copy.12), calls=%async_computation | async-start | bytes 393216 | tf_op jit(solution)/shard_map/all_to_all | solution.py:75
  46.5 30.9 %all-gather.1 = bf16[8,4,3072]{2,1,0:T(4,128)(2,1)S(1)} all-gather(bf16[1,4,3072]{2,1,0:T(4,128)(2,1)} %bitcast.28), channel_id=1, replica_groups=mesh['dp'=4,'mp'=8] {'mp'}, dimensions={0}, use_global_device_ids=true | all-gather | bytes 221184 | tf_op jit(solution)/shard_map/all_gather | solution.py:40
  77.5 5.5 %multiply_convert_fusion = (bf16[32,1536]{1,0:T(8,128)(2,1)S(1)}, f32[32,1536]{1,0:T(8,128)S(1)}) fusion(bf16[32,3072]{1,0:T(8,128)(2,1)S(1)} %reshape.47, bf16[3072,1536]{1,0:T(8,128)(2,1)} %param.6), kind=kOutput, calls=%fused_computation.13 | convolution fusion | flops 302235648 | bytes 9928704 | tf_op jit(solution)/shard_map/dot_general | solution.py:42
  83.0 6.7 %fusion = bf16[32,1536]{1,0:T(8,128)(2,1)S(1)} fusion(bf16[32,3072]{1,0:T(8,128)(2,1)S(1)} %reshape.49, bf16[1536,3072]{1,0:T(8,128)(2,1)} %param.7, f32[32,1536]{1,0:T(8,128)S(1)} %get-tuple-element.11), kind=kOutput, calls=%fused_computation.5 | convolution fusion | flops 302481408 | bytes 9928704 | tf_op jit(solution)/shard_map/dot_general | solution.py:52
  89.8 3.5 %convolution_convert_fusion.2 = bf16[32,3072]{1,0:T(8,128)(2,1)} fusion(bf16[32,1536]{1,0:T(8,128)(2,1)S(1)} %fusion, bf16[3072,1536]{1,0:T(8,128)(2,1)S(1)} %bitcast.23), kind=kOutput, calls=%fused_computation.2 | convolution fusion | flops 302088192 | bytes 9732096 | tf_op jit(solution)/shard_map/dot_general | solution.py:57
  93.3 2.4 %convolution_convert_fusion.3 = bf16[32,3072]{1,0:T(8,128)(2,1)} fusion(bf16[32,1536]{1,0:T(8,128)(2,1)S(1)} %get-tuple-element.10, bf16[1536,3072]{1,0:T(8,128)(2,1)S(1)} %bitcast.25), kind=kOutput, calls=%fused_computation.3 | convolution fusion | flops 302088192 | bytes 9732096 | tf_op jit(solution)/shard_map/dot_general | solution.py:46
  95.8 0.1 all_to_all.27
  95.9 6.9 %all_gather.15 = bf16[128,1536]{1,0:T(8,128)(2,1)S(1)} all-gather(bf16[32,1536]{1,0:T(8,128)(2,1)S(1)} %get-tuple-element.10), channel_id=1, replica_groups=mesh['dp'=4,'mp'=8] {'dp'}, dimensions={0}, use_global_device_ids=true | all-gather | bytes 491520 | tf_op jit(solution)/shard_map/all_gather | solution.py:79
  102.7 0.7 copy.13
  103.4 0.6 dynamic-slice
  104.6 6.6 %all_gather.14 = bf16[128,1536]{1,0:T(8,128)(2,1)S(1)} all-gather(bf16[32,1536]{1,0:T(8,128)(2,1)S(1)} %fusion), channel_id=1, replica_groups=mesh['dp'=4,'mp'=8] {'dp'}, dimensions={0}, use_global_device_ids=true | all-gather | bytes 491520 | tf_op jit(solution)/shard_map/all_gather | solution.py:80
  111.2 3.5 %all-to-all-start.1 = ((bf16[32,4,768]{2,0,1:T(8,128)(2,1)}), bf16[32,4,768]{2,0,1:T(8,128)(2,1)S(1)}, u32[]{:S(2)}, u32[]{:S(2)}) async-start(bf16[32,4,768]{2,0,1:T(8,128)(2,1)} %copy.13), calls=%async_computation.1 | async-start | bytes 393216 | tf_op jit(solution)/shard_map/all_to_all | solution.py:76
  114.8 5.1 %convolution_convert_fusion.1 = bf16[4,768,1536]{2,1,0:T(8,128)(2,1)} fusion(bf16[4,32,1536]{2,1,0:T(8,128)(2,1)S(1)} %bitcast.27, bf16[32,4,768]{2,0,1:T(8,128)(2,1)S(1)} %all-to-all-done), kind=kOutput, calls=%fused_computation.1 | convolution fusion | flops 306708480 | bytes 10027008 | tf_op jit(solution)/shard_map/nta,ntb->nab/dot_general | solution.py:28
  119.9 5.1 %convolution_convert_fusion = bf16[4,1536,768]{2,1,0:T(8,128)(2,1)} fusion(bf16[4,32,1536]{2,1,0:T(8,128)(2,1)S(1)} %bitcast.26, bf16[32,4,768]{2,0,1:T(8,128)(2,1)S(1)} %all-to-all-done.1), kind=kOutput, calls=%fused_computation | convolution fusion | flops 306708480 | bytes 10027008 | tf_op jit(solution)/shard_map/nta,ntb->nab/dot_general | solution.py:28
  125.0 7.3 %reduce_sum.64 = bf16[768,1536]{1,0:T(8,128)(2,1)} reduce(bf16[4,768,1536]{2,1,0:T(8,128)(2,1)} %convolution_convert_fusion.1, bf16[]{:T(256)} %constant.22.clone.1), dimensions={0}, to_apply=%region_6.0 | reduce | flops 3538944 | bytes 11796482 | tf_op jit(solution)/shard_map/reduce_sum | solution.py:32
  132.3 7.1 %reduce_sum.65 = bf16[1536,768]{1,0:T(8,128)(2,1)} reduce(bf16[4,1536,768]{2,1,0:T(8,128)(2,1)} %convolution_convert_fusion, bf16[]{:T(256)} %constant.22.clone.1), dimensions={0}, to_apply=%region_7.0 | reduce | flops 3538944 | bytes 11796482 | tf_op jit(solution)/shard_map/reduce_sum | solution.py:32
  139.4 29.3 %all-reduce.5.cloned.1.call-done = (bf16[32,3072]{1,0:T(8,128)(2,1)}, bf16[32,3072]{1,0:T(8,128)(2,1)}) async-done(((bf16[32,3072]{1,0:T(8,128)(2,1)}, bf16[32,3072]{1,0:T(8,128)(2,1)}), (bf16[32,3072]{1,0:T(8,128)(2,1)}, bf16[32,3072]{1,0:T(8,128)(2,1)})) %all-reduce.5.cloned.1.call-update) | async-done | bytes 393232
  168.7 1.0 convert_reduce_fusion
  169.8 1.5 fusion.14
  (30 shorter events, 0.3 us)
Async XLA Ops:
  43.0 68.2 %all-to-all-start = ((bf16[32,4,768]{2,0,1:T(8,128)(2,1)}), bf16[32,4,768]{2,0,1:T(8,128)(2,1)S(1)}, u32[]{:S(2)}, u32[]{:S(2)}) async-start(bf16[32,4,768]{2,0,1:T(8,128)(2,1)} %copy.12), calls=%async_computation | async-start | bytes 393216 | tf_op jit(solution)/shard_map/all_to_all | solution.py:75
  46.4 122.3 %all-reduce.5.cloned.1.call-start = ((), (), s32[]{:S(2)}) async-start(), calls=%async_computation.2 | async-start | bytes 786432
  77.5 12.3 %slice-start = ((s8[9437184]{0:T(1024)(128)(4,1)}), s8[4194304]{0:T(1024)(128)(4,1)S(1)}, s32[]{:S(2)}) async-start(s8[9437184]{0:T(1024)(128)(4,1)} %bitcast.22), calls=%async_computation.3 | async-start | bytes 8388608
  77.5 12.3 %slice-start.1 = ((s8[9437184]{0:T(1024)(128)(4,1)}), s8[4194304]{0:T(1024)(128)(4,1)S(1)}, s32[]{:S(2)}) async-start(s8[9437184]{0:T(1024)(128)(4,1)} %bitcast.22), calls=%async_computation.4 | async-start | bytes 8388608
  83.0 6.8 %slice-start.2 = ((s8[9437184]{0:T(1024)(128)(4,1)}), s8[1048576]{0:T(1024)(128)(4,1)S(1)}, s32[]{:S(2)}) async-start(s8[9437184]{0:T(1024)(128)(4,1)} %bitcast.22), calls=%async_computation.5 | async-start | bytes 2097152
  83.0 10.3 %slice-start.3 = ((s8[9437184]{0:T(1024)(128)(4,1)}), s8[4194304]{0:T(1024)(128)(4,1)S(1)}, s32[]{:S(2)}) async-start(s8[9437184]{0:T(1024)(128)(4,1)} %bitcast.24), calls=%async_computation.6 | async-start | bytes 8388608
  83.0 10.3 %slice-start.4 = ((s8[9437184]{0:T(1024)(128)(4,1)}), s8[4194304]{0:T(1024)(128)(4,1)S(1)}, s32[]{:S(2)}) async-start(s8[9437184]{0:T(1024)(128)(4,1)} %bitcast.24), calls=%async_computation.7 | async-start | bytes 8388608
  89.8 3.5 %slice-start.5 = ((s8[9437184]{0:T(1024)(128)(4,1)}), s8[1048576]{0:T(1024)(128)(4,1)S(1)}, s32[]{:S(2)}) async-start(s8[9437184]{0:T(1024)(128)(4,1)} %bitcast.24), calls=%async_computation.8 | async-start | bytes 2097152
  93.3 10.1 %copy-start.2 = (u32[32]{0:T(128)S(1)}, u32[32]{0:T(128)}, u32[]{:S(2)}) copy-start(u32[32]{0:T(128)} %constant.27) | copy-start | bytes 388
  111.2 8.7 %all-to-all-start.1 = ((bf16[32,4,768]{2,0,1:T(8,128)(2,1)}), bf16[32,4,768]{2,0,1:T(8,128)(2,1)S(1)}, u32[]{:S(2)}, u32[]{:S(2)}) async-start(bf16[32,4,768]{2,0,1:T(8,128)(2,1)} %copy.13), calls=%async_computation.1 | async-start | bytes 393216 | tf_op jit(solution)/shard_map/all_to_all | solution.py:76
  125.0 43.7 %copy-start = (bf16[4,3072]{1,0:T(4,128)(2,1)S(1)}, bf16[4,3072]{1,0:T(4,128)(2,1)}, u32[]{:S(2)}) copy-start(bf16[4,3072]{1,0:T(4,128)(2,1)} %param.4) | copy-start | bytes 73732
  125.0 44.7 %copy-start.1 = (bf16[4,3072]{1,0:T(4,128)(2,1)S(1)}, bf16[4,3072]{1,0:T(4,128)(2,1)}, u32[]{:S(2)}) copy-start(bf16[4,3072]{1,0:T(4,128)(2,1)} %param.5) | copy-start | bytes 73732
Sparse Core Ops, SparseCore 0:
  95.9 72.7 all-reduce.4
where the time goes:
time: 179 us; the launch traced here: 178 us
  blocking collectives  76.7 us (43%)
  waiting for transfers between devices  29.3 us (16%)
  matrix products  28.4 us (16%)
  other arithmetic  19.7 us (11%)
  between operations  14.9 us (8%)
  starting transfers between devices  6.95 us (4%)
  local copies, waits for them, and re-layouts  2.29 us (1%)
    all_gather x1, blocking collectives, body(): lax.all_gather(standardised_input, 'mp', axis=0, tiled=True)  32.4 us
    all_gather x1, blocking collectives, body(): lax.all_gather(cotangent, 'mp', axis=0, tiled=True)  30.9 us
    unnamed x2, waiting for transfers between devices  29.3 us
    reduce_sum x2, other arithmetic, shard_sum(): return jnp.sum(per_shard, axis=0)  14.4 us
    dot_general x2, matrix products, shard_sum(): jnp.einsum('nta,ntb->nab', left_blocks, right_blocks, preferred_element_t...  10.2 us
    all_gather x1, blocking collectives, body(): lax.all_gather(hidden, 'dp', axis=0, tiled=True)  6.86 us
    dot_general x1, matrix products, body(): lax.dot_general(cot_all, down_weight, (((1,), (1,)), ((), ())), preferred...  6.72 us
    all_gather x1, blocking collectives, body(): lax.all_gather(act_grad, 'dp', axis=0, tiled=True)  6.58 us
  transfers between devices with their start and end apart: 3, of which 1 were waited for; matrix products, arithmetic and copies ran while one was open for 25% of the time, Pallas kernels for 0%

commit v1 on v0

v1 whole, which is shorter than its diff:
```python
import functools

import jax
import jax.numpy as jnp
from jax import lax
from jax.experimental import pallas as pl
from jax.experimental.pallas import tpu as pltpu
from jax.sharding import PartitionSpec as P

ROOT_HALF = 0.7071067811865476
DENSITY_SCALE = 0.3989422804014327
TILE_ROWS = 16
MESH = pl.DeviceIdType.MESH
F32 = jnp.float32
BF16 = jnp.bfloat16


def chunk_of(size, choices=(512, 384, 256)):
    for choice in choices:
        if size % choice == 0:
            return choice
    return size


def dot(left, right, left_dim=1, right_dim=0):
    return lax.dot_general(
        left, right, (((left_dim,), (right_dim,)), ((), ())), preferred_element_type=F32
    )


def one_hot(shape, wanted):
    return jnp.where(wanted, 1.0, 0.0).astype(BF16)


def kernel(
    n_dp, n_mp,
    tokens_ref, cot_ref, up_hbm, down_hbm,
    mixed_ref, tgrad_ref, up_grad_hbm, down_grad_hbm,
    up_v, down_v,
    gather_n, gather_c,
    rs_out_send, rs_out, rs_grad_send, rs_grad,
    ncol_send, ccol_send, ncol, ccol,
    hid, act, slope, rows_n, rows_c,
    up_out, down_out,
    load_sem, out_sem, mp_send, mp_recv, dp_send, dp_recv,
):
    rows, width = tokens_ref.shape
    pieces = TILE_ROWS // rows
    wide = width // pieces
    shard_rows = rows * n_mp
    packed_rows = TILE_ROWS * n_mp
    units = up_v.shape[1]
    feats = width // n_dp
    dp = lax.axis_index("dp")
    mp = lax.axis_index("mp")

    def dp_peer(o):
        return {"dp": lax.rem(dp + o, n_dp), "mp": mp}

    def mp_peer(o):
        return {"dp": dp, "mp": lax.rem(mp + o, n_mp)}

    loads = []
    parts = load_sem.shape[1]
    for w, (src, dst) in enumerate(((up_hbm, up_v), (down_hbm, down_v))):
        step = src.shape[0] // parts
        for i in range(parts):
            where = pl.ds(i * step, step)
            copy = pltpu.make_async_copy(src.at[where], dst.at[where], load_sem.at[w, i])
            copy.start()
            loads.append(copy)

    barrier = pltpu.get_barrier_semaphore()
    for o in range(1, n_mp):
        pl.semaphore_signal(barrier, inc=1, device_id=mp_peer(o), device_id_type=MESH)
    for o in range(1, n_dp):
        pl.semaphore_signal(barrier, inc=1, device_id=dp_peer(o), device_id_type=MESH)

    sent = []

    def send_mp(kind, src, dst, o):
        copy = pltpu.make_async_remote_copy(
            src_ref=src, dst_ref=dst,
            send_sem=mp_send.at[kind, o], recv_sem=mp_recv.at[kind, o],
            device_id=mp_peer(o), device_id_type=MESH,
        )
        copy.start()
        sent.append(copy)
        return copy

    def send_dp(kind, src, dst, o):
        copy = pltpu.make_async_remote_copy(
            src_ref=src, dst_ref=dst,
            send_sem=dp_send.at[kind, o], recv_sem=dp_recv.at[kind, o],
            device_id=dp_peer(o), device_id_type=MESH,
        )
        copy.start()
        sent.append(copy)
        return copy

    tokens = tokens_ref[...].astype(F32)
    centred = tokens - jnp.mean(tokens, axis=1, keepdims=True)
    variance = jnp.mean(centred * centred, axis=1, keepdims=True)
    inverse = lax.rsqrt(variance + 1e-06)
    xhat = centred * inverse
    cot = cot_ref[...].astype(F32)

    def pack(values):
        return jnp.concatenate(
            [values[:, q * wide:(q + 1) * wide] for q in range(pieces)], axis=0
        ).astype(BF16)

    gather_n[0] = pack(xhat)
    gather_c[0] = pack(cot)

    pl.semaphore_wait(barrier, n_mp - 1 + n_dp - 1)
    got_n = [send_mp(0, gather_n.at[0], gather_n.at[o], o) for o in range(1, n_mp)]
    got_c = [send_mp(1, gather_c.at[0], gather_c.at[o], o) for o in range(1, n_mp)]

    at = lax.broadcasted_iota(jnp.int32, (shard_rows, packed_rows), 0)
    to = lax.broadcasted_iota(jnp.int32, (shard_rows, packed_rows), 1)
    home = at + (at // rows) * (TILE_ROWS - rows)
    unpackers = [one_hot(None, to == home + q * rows) for q in range(pieces)]
    at = lax.broadcasted_iota(jnp.int32, (8, packed_rows), 0)
    to = lax.broadcasted_iota(jnp.int32, (8, packed_rows), 1) % TILE_ROWS
    adders = [one_hot(None, (to == at + q * rows) & (at < rows)) for q in range(pieces)]

    def unpack(gathered, out):
        flat = gathered[...].reshape(packed_rows, wide)
        for q in range(pieces):
            out[:, q * wide:(q + 1) * wide] = dot(unpackers[q], flat).astype(BF16)

    def send_columns(kind, out, blocks, slots):
        for j in range(n_dp):
            blocks[j] = out[:, j * feats:(j + 1) * feats]
        got = [
            send_dp(kind, blocks.at[lax.rem(dp + o, n_dp)], slots.at[o], o)
            for o in range(1, n_dp)
        ]
        slots[0] = blocks[dp]
        return got

    for copy in got_n:
        copy.wait_recv()
    unpack(gather_n, rows_n)
    got_ncol = send_columns(0, rows_n, ncol_send, ncol)

    for copy in loads[:parts]:
        copy.wait()
    step = chunk_of(units)
    for i in range(units // step):
        cols = slice(i * step, (i + 1) * step)
        pre_act = dot(rows_n[...], up_v[:, cols])
        cumulative = 0.5 * (1.0 + lax.erf(pre_act * ROOT_HALF))
        density = jnp.exp(-0.5 * pre_act * pre_act) * DENSITY_SCALE
        hid[0, :, cols] = (pre_act * cumulative).astype(BF16)
        slope[:, cols] = cumulative + pre_act * density
    got_hid = [send_dp(2, hid.at[0], hid.at[o], o) for o in range(1, n_dp)]

    for copy in got_c:
        copy.wait_recv()
    unpack(gather_c, rows_c)
    got_ccol = send_columns(1, rows_c, ccol_send, ccol)

    for copy in loads[parts:]:
        copy.wait()

    def scatter(kind, partial_of, send, slots):
        total = jnp.zeros((packed_rows, wide), F32)
        for q in range(pieces):
            total += dot(unpackers[q], partial_of(q).astype(BF16), 0, 0)
        send[...] = total.astype(BF16).reshape(n_mp, TILE_ROWS, wide)
        got = [
            send_mp(kind, send.at[n_mp - o], slots.at[o], o) for o in range(1, n_mp)
        ]
        slots[0] = send[0]
        return got

    got_out = scatter(
        2, lambda q: dot(hid[0], down_v[:, q * wide:(q + 1) * wide]), rs_out_send, rs_out
    )

    for i in range(units // step):
        cols = slice(i * step, (i + 1) * step)
        hidden_grad = dot(rows_c[...], down_v[cols, :], 1, 1)
        act[0, :, cols] = (hidden_grad * slope[:, cols]).astype(BF16)
    got_act = [send_dp(3, act.at[0], act.at[o], o) for o in range(1, n_dp)]

    got_grad = scatter(
        3, lambda q: dot(act[0], up_v[q * wide:(q + 1) * wide, :], 1, 1), rs_grad_send, rs_grad
    )

    stores = []

    def weight_grad(left, right, out, out_hbm, which):
        lefts = left.shape[2]
        step = chunk_of(lefts)
        right_rows = right[...].reshape(n_dp * shard_rows, right.shape[2])
        for i in range(lefts // step):
            cols = slice(i * step, (i + 1) * step)
            left_rows = left[:, :, cols].reshape(n_dp * shard_rows, step)
            out[cols, :] = dot(left_rows, right_rows, 0, 0).astype(BF16)
            copy = pltpu.make_async_copy(out.at[cols], out_hbm.at[cols], out_sem.at[which, i])
            copy.start()
            stores.append(copy)

    for copy in got_ccol + got_hid:
        copy.wait_recv()
    weight_grad(hid, ccol, down_out, down_grad_hbm, 0)
    for copy in got_ncol + got_act:
        copy.wait_recv()
    weight_grad(ncol, act, up_out, up_grad_hbm, 1)

    def summed(got, slots):
        for copy in got:
            copy.wait_recv()
        flat = slots[...].reshape(packed_rows, wide)
        return jnp.concatenate([dot(adders[q], flat)[:rows] for q in range(pieces)], axis=1)

    block_out = summed(got_out, rs_out)
    mixed_ref[...] = (tokens + block_out).astype(BF16)
    grad = summed(got_grad, rs_grad)
    grad_mean = jnp.mean(grad, axis=1, keepdims=True)
    projection = jnp.mean(grad * xhat, axis=1, keepdims=True)
    tgrad_ref[...] = (cot + inverse * (grad - grad_mean - xhat * projection)).astype(BF16)

    for copy in stores:
        copy.wait()
    for copy in sent:
        copy.wait_send()


def body(n_dp, n_mp, tokens, cotangent, up_weight, down_weight):
    rows, width = tokens.shape
    units = up_weight.shape[1]
    feats = width // n_dp
    shard_rows = rows * n_mp
    wide = width * rows // TILE_ROWS
    packed = pltpu.VMEM((n_mp, TILE_ROWS, wide), BF16)
    columns = pltpu.VMEM((n_dp, shard_rows, feats), BF16)
    hiddens = pltpu.VMEM((n_dp, shard_rows, units), BF16)
    macs = 4 * shard_rows * width * units + 2 * n_dp * shard_rows * units * feats
    return pl.pallas_call(
        functools.partial(kernel, n_dp, n_mp),
        out_shape=(
            jax.ShapeDtypeStruct(tokens.shape, BF16),
            jax.ShapeDtypeStruct(tokens.shape, BF16),
            jax.ShapeDtypeStruct((feats, units), BF16),
            jax.ShapeDtypeStruct((units, feats), BF16),
        ),
        in_specs=[pl.BlockSpec(memory_space=pltpu.VMEM)] * 2
        + [pl.BlockSpec(memory_space=pl.ANY)] * 2,
        out_specs=[pl.BlockSpec(memory_space=pltpu.VMEM)] * 2
        + [pl.BlockSpec(memory_space=pl.ANY)] * 2,
        scratch_shapes=[
            pltpu.VMEM(up_weight.shape, BF16),
            pltpu.VMEM(down_weight.shape, BF16),
            packed, packed,
            packed, packed, packed, packed,
            columns, columns, columns, columns,
            hiddens, hiddens,
            pltpu.VMEM((shard_rows, units), F32),
            pltpu.VMEM((shard_rows, width), BF16),
            pltpu.VMEM((shard_rows, width), BF16),
            pltpu.VMEM((feats, units), BF16),
            pltpu.VMEM((units, feats), BF16),
            pltpu.SemaphoreType.DMA((2, 4)),
            pltpu.SemaphoreType.DMA((2, 8)),
            pltpu.SemaphoreType.DMA((4, n_mp)),
            pltpu.SemaphoreType.DMA((4, n_mp)),
            pltpu.SemaphoreType.DMA((4, n_dp)),
            pltpu.SemaphoreType.DMA((4, n_dp)),
        ],
        compiler_params=pltpu.CompilerParams(
            collective_id=0, has_side_effects=True, vmem_limit_bytes=56 * 1024 * 1024
        ),
        cost_estimate=pl.CostEstimate(
            flops=2 * macs, bytes_accessed=4 * width * units, transcendentals=2 * shard_rows * units
        ),
    )(tokens, cotangent, up_weight, down_weight)


def solution(mesh):
    return jax.shard_map(
        functools.partial(body, mesh.shape["dp"], mesh.shape["mp"]),
        mesh=mesh,
        in_specs=(P(("dp", "mp"), None), P(("dp", "mp"), None), P(None, "mp"), P("mp", None)),
        out_specs=(P(("dp", "mp"), None), P(("dp", "mp"), None), P("dp", "mp"), P("mp", "dp")),
        check_vma=False,
    )
```

time: 179 us -> 41.5 us (0.23)
  blocking collectives: 76.7 us -> 0 us
  Pallas kernels: 0 us -> 33 us
  waiting for transfers between devices: 29.3 us -> 0 us
  matrix products: 28.4 us -> 0 us
  other arithmetic: 19.7 us -> 0 us
  between operations: 14.9 us -> 0.64 us
  starting transfers between devices: 6.95 us -> 0 us
  local copies, waits for them, and re-layouts: 2.29 us -> 7.49 us
    all_gather x4 -> x0, blocking collectives: 76.7 us -> none  [the longest x1 32.4 us: body(): lax.all_gather(standardised_input, 'mp', axis=0, tiled=True)]
    pallas_call x0 -> x1, Pallas kernels: none -> 33 us  [body(): pl.pallas_call(functools.partial(kernel, n_dp, n_mp), out_shape=(jax.Shap...]
    unnamed x2 -> x0, waiting for transfers between devices: 29.3 us -> none
    dot_general x6 -> x0, matrix products: 28.4 us -> none  [the longest x2 10.2 us: shard_sum(): jnp.einsum('nta,ntb->nab', left_blocks, right_blocks, preferred_element_t...]
    reduce_sum x5 -> x0, other arithmetic: 17.3 us -> none  [the longest x2 14.4 us: shard_sum(): return jnp.sum(per_shard, axis=0)]
    all_to_all x2 -> x0, starting transfers between devices: 6.91 us -> none  [the longest x1 3.55 us: body(): lax.all_to_all(cot_all, 'dp', split_axis=1, concat_axis=0, tiled=True)]
    unnamed x21 -> x6, local copies, waits for them, and re-layouts: 0.74 us -> 7.49 us
  transfers between devices with their start and end apart: 3 -> 0, of which waited for: 1 -> 0; matrix products, arithmetic and copies ran while one was open for 25% -> 0% of each run, Pallas kernels for 0% -> 0%
where the time goes in v1:
time: 41.5 us; the launch traced here: 41.2 us
  Pallas kernels  33 us (80%)
  local copies, waits for them, and re-layouts  7.49 us (18%)
  between operations  0.64 us (2%)
    pallas_call x1, Pallas kernels, body(): pl.pallas_call(functools.partial(kernel, n_dp, n_mp), out_shape=(jax.Shap...  33 us
    unnamed x6, local copies, waits for them, and re-layouts  7.49 us

profile of v1, /device:TPU:0, one launch (start us, length us, event | category | flops | bytes accessed | tf_op | source)
XLA Modules:
  0.0 41.2 jit_solution(9509548442593252393)
XLA Ops:
  0.6 33.0 %shard_map.75 = (bf16[4,3072]{1,0:T(4,128)(2,1)}, bf16[4,3072]{1,0:T(4,128)(2,1)}, bf16[768,1536]{1,0:T(8,128)(2,1)}, bf16[1536,768]{1,0:T(8,128)(2,1)}) custom-call(bf16[4,3072]{1,0:T(4,128)(2,1)} %tokens_ref.1, bf16[4,3072]{1,0:T(4,128)(2,1)} %cot_ref.1, bf16[3072,1536]{1,0:T(8,128)(2,1)} %up_hbm.1, bf16[1536,3072]{1,0:T(8,128)(2,1)} %down_hbm.1), custom_call_target="tpu_custom_call" | custom-call | flops 1811939328 | bytes 18874368 | tf_op jit(solution)/shard_map/pallas_call | solution.py:243
  33.7 1.4 %copy.12 = bf16[4,3072]{1,0:T(4,128)(2,1)} copy(bf16[4,3072]{1,0:T(4,128)(2,1)} %get-tuple-element.8) | data formatting | bytes 49152
  35.0 1.4 %copy.13 = bf16[4,3072]{1,0:T(4,128)(2,1)} copy(bf16[4,3072]{1,0:T(4,128)(2,1)} %get-tuple-element.9) | data formatting | bytes 49152
  36.4 0.0 copy-start
  36.4 3.4 %copy.14 = bf16[768,1536]{1,0:T(8,128)(2,1)} copy(bf16[768,1536]{1,0:T(8,128)(2,1)} %get-tuple-element.10) | data formatting | bytes 4718592
  39.8 0.0 copy-done
  39.8 1.4 %copy.15 = bf16[1536,768]{1,0:T(8,128)(2,1)} copy(bf16[1536,768]{1,0:T(8,128)(2,1)S(1)} %copy-done) | data formatting | bytes 4718592
Async XLA Ops:
  36.4 3.4 %copy-start = (bf16[1536,768]{1,0:T(8,128)(2,1)S(1)}, bf16[1536,768]{1,0:T(8,128)(2,1)}, u32[]{:S(2)}) copy-start(bf16[1536,768]{1,0:T(8,128)(2,1)} %get-tuple-element.11) | copy-start | bytes 7077892

commit v2 on v1

v2 whole, which is shorter than its diff:
```python
import functools

import jax
import jax.numpy as jnp
from jax import lax
from jax.experimental import pallas as pl
from jax.experimental.pallas import tpu as pltpu
from jax.sharding import PartitionSpec as P

ROOT_HALF = 0.7071067811865476
DENSITY_SCALE = 0.3989422804014327
TILE_ROWS = 16
MESH = pl.DeviceIdType.MESH
F32 = jnp.float32
BF16 = jnp.bfloat16


def chunk_of(size, choices=(512, 384, 256)):
    for choice in choices:
        if size % choice == 0:
            return choice
    return size


def dot(left, right, left_dim=1, right_dim=0):
    return lax.dot_general(
        left, right, (((left_dim,), (right_dim,)), ((), ())), preferred_element_type=F32
    )


def one_hot(wanted):
    return jnp.where(wanted, 1.0, 0.0).astype(BF16)


def relay_group(axis, n, send_sem, recv_sem, sent):
    other_axis = "mp" if axis == "dp" else "dp"
    me, fixed = lax.axis_index(axis), lax.axis_index(other_axis)
    lines = n // 2
    line, side = me // 2, me % 2

    def peer(block):
        to_line = lax.rem(line + block // 2, lines)
        to_side = side if block % 2 == 0 else 1 - side
        return {axis: 2 * to_line + to_side, other_axis: fixed}

    def start(kind, src, dst, block, to=None):
        copy = pltpu.make_async_remote_copy(
            src_ref=src, dst_ref=dst,
            send_sem=send_sem.at[kind, block], recv_sem=recv_sem.at[kind, block],
            device_id=peer(block if to is None else to), device_id_type=MESH,
        )
        copy.start()
        sent.append(copy)
        return copy

    def spread(kind, src, slots):
        straight = [start(kind, src, slots.at[2 * k], 2 * k) for k in range(1, lines)]
        return straight, [start(kind, src, slots.at[1], 1)]

    def pass_on(kind, slots, straight, crossed):
        for k in range(1, lines):
            straight[k - 1].wait_recv()
            crossed.append(start(kind, slots.at[2 * k], slots.at[2 * k + 1], 2 * k + 1, to=1))

    def opposite(block):
        return 2 * ((lines - block // 2) % lines) + block % 2

    return peer, start, spread, pass_on, opposite


def row_norm(tokens):
    centred = tokens - jnp.mean(tokens, axis=1, keepdims=True)
    variance = jnp.mean(centred * centred, axis=1, keepdims=True)
    inverse = lax.rsqrt(variance + 1e-06)
    return centred * inverse, inverse


def exchange_kernel(
    n_dp, n_mp,
    tokens_ref, cot_ref, up_hbm, down_hbm,
    rs_out, rs_grad, ncol, ccol, hid, act,
    up_v, down_v,
    gather_n, gather_c, rs_out_send, rs_grad_send,
    ncol_send, ccol_send, hid_own, act_own, slope, rows_n, rows_c,
    load_sem, own_sem, mp_send, mp_recv, dp_send, dp_recv,
):
    rows, width = tokens_ref.shape
    pieces = TILE_ROWS // rows
    wide = width // pieces
    shard_rows = rows * n_mp
    packed_rows = TILE_ROWS * n_mp
    units = up_v.shape[1]
    feats = width // n_dp

    loads = []
    parts = load_sem.shape[1]
    for w, (src, dst) in enumerate(((up_hbm, up_v), (down_hbm, down_v))):
        step = src.shape[0] // parts
        for i in range(parts):
            where = pl.ds(i * step, step)
            copy = pltpu.make_async_copy(src.at[where], dst.at[where], load_sem.at[w, i])
            copy.start()
            loads.append(copy)

    sent = []
    mp_peer, mp_start, mp_spread, mp_pass_on, mp_opposite = relay_group(
        "mp", n_mp, mp_send, mp_recv, sent
    )
    dp_peer, dp_start, dp_spread, dp_pass_on, dp_opposite = relay_group(
        "dp", n_dp, dp_send, dp_recv, sent
    )
    barrier = pltpu.get_barrier_semaphore()
    for b in range(1, n_mp):
        pl.semaphore_signal(barrier, inc=1, device_id=mp_peer(b), device_id_type=MESH)
    for b in range(1, n_dp):
        pl.semaphore_signal(barrier, inc=1, device_id=dp_peer(b), device_id_type=MESH)

    def pack(values):
        return jnp.concatenate(
            [values[:, q * wide:(q + 1) * wide] for q in range(pieces)], axis=0
        ).astype(BF16)

    xhat, _ = row_norm(tokens_ref[...].astype(F32))
    gather_n[0] = pack(xhat)
    gather_c[0] = pack(cot_ref[...].astype(F32))

    pl.semaphore_wait(barrier, n_mp - 1 + n_dp - 1)
    straight_n, crossed_n = mp_spread(0, gather_n.at[0], gather_n)
    straight_c, crossed_c = mp_spread(1, gather_c.at[0], gather_c)

    at = lax.broadcasted_iota(jnp.int32, (shard_rows, packed_rows), 0)
    to = lax.broadcasted_iota(jnp.int32, (shard_rows, packed_rows), 1)
    home = at + (at // rows) * (TILE_ROWS - rows)
    unpackers = [one_hot(to == home + q * rows) for q in range(pieces)]

    def unpack(gathered, out):
        flat = gathered[...].reshape(packed_rows, wide)
        for q in range(pieces):
            out[:, q * wide:(q + 1) * wide] = dot(unpackers[q], flat).astype(BF16)

    own = []

    def keep(src, slots, which):
        copy = pltpu.make_async_copy(src, slots.at[0], own_sem.at[which])
        copy.start()
        own.append(copy)

    def send_columns(kind, out, blocks, slots):
        for j in range(n_dp):
            blocks[j] = out[:, j * feats:(j + 1) * feats]
        got = [
            dp_start(kind, blocks.at[dp_peer(b)["dp"]], slots.at[b], b) for b in range(1, n_dp)
        ]
        keep(blocks.at[lax.axis_index("dp")], slots, kind)
        return got

    mp_pass_on(0, gather_n, straight_n, crossed_n)
    mp_pass_on(1, gather_c, straight_c, crossed_c)
    for copy in crossed_n:
        copy.wait_recv()
    unpack(gather_n, rows_n)
    arrivals = send_columns(0, rows_n, ncol_send, ncol)

    for copy in loads[:parts]:
        copy.wait()
    step = chunk_of(units)
    for i in range(units // step):
        cols = slice(i * step, (i + 1) * step)
        pre_act = dot(rows_n[...], up_v[:, cols])
        cumulative = 0.5 * (1.0 + lax.erf(pre_act * ROOT_HALF))
        density = jnp.exp(-0.5 * pre_act * pre_act) * DENSITY_SCALE
        hid_own[:, cols] = (pre_act * cumulative).astype(BF16)
        slope[:, cols] = cumulative + pre_act * density
    straight_h, crossed_h = dp_spread(2, hid_own, hid)
    keep(hid_own, hid, 2)

    for copy in crossed_c:
        copy.wait_recv()
    unpack(gather_c, rows_c)
    arrivals += send_columns(1, rows_c, ccol_send, ccol)

    for copy in loads[parts:]:
        copy.wait()

    def scatter(kind, partial_of, send, slots):
        total = jnp.zeros((packed_rows, wide), F32)
        for q in range(pieces):
            total += dot(unpackers[q], partial_of(q).astype(BF16), 0, 0)
        send[...] = total.astype(BF16).reshape(n_mp, TILE_ROWS, wide)
        got = [mp_start(kind, send.at[mp_opposite(b)], slots.at[b], b) for b in range(1, n_mp)]
        keep(send.at[0], slots, 2 + kind)
        return got

    arrivals += scatter(
        2, lambda q: dot(hid_own[...], down_v[:, q * wide:(q + 1) * wide]), rs_out_send, rs_out
    )
    for i in range(units // step):
        cols = slice(i * step, (i + 1) * step)
        hidden_grad = dot(rows_c[...], down_v[cols, :], 1, 1)
        act_own[:, cols] = (hidden_grad * slope[:, cols]).astype(BF16)
    straight_a, crossed_a = dp_spread(3, act_own, act)
    keep(act_own, act, 3)
    dp_pass_on(2, hid, straight_h, crossed_h)
    arrivals += scatter(
        3, lambda q: dot(act_own[...], up_v[q * wide:(q + 1) * wide, :], 1, 1), rs_grad_send, rs_grad
    )
    dp_pass_on(3, act, straight_a, crossed_a)

    for copy in arrivals + crossed_h + crossed_a:
        copy.wait_recv()
    for copy in own:
        copy.wait()
    for copy in sent:
        copy.wait_send()


def result_kernel(
    tokens_ref, cot_ref, rs_out, rs_grad, ncol, ccol, hid, act,
    mixed_ref, tgrad_ref, up_grad_hbm, down_grad_hbm,
    up_out, down_out, out_sem,
):
    rows, width = tokens_ref.shape
    pieces = TILE_ROWS // rows
    n_mp, _, wide = rs_out.shape
    packed_rows = TILE_ROWS * n_mp
    stores = []

    def weight_grad(left, right, out, out_hbm, which):
        n_dp, shard_rows, lefts = left.shape
        step = chunk_of(lefts)
        right_rows = right[...].reshape(n_dp * shard_rows, right.shape[2])
        for i in range(lefts // step):
            cols = slice(i * step, (i + 1) * step)
            left_rows = left[:, :, cols].reshape(n_dp * shard_rows, step)
            out[cols, :] = dot(left_rows, right_rows, 0, 0).astype(BF16)
            copy = pltpu.make_async_copy(out.at[cols], out_hbm.at[cols], out_sem.at[which, i])
            copy.start()
            stores.append(copy)

    weight_grad(hid, ccol, down_out, down_grad_hbm, 0)
    weight_grad(ncol, act, up_out, up_grad_hbm, 1)

    at = lax.broadcasted_iota(jnp.int32, (8, packed_rows), 0)
    to = lax.broadcasted_iota(jnp.int32, (8, packed_rows), 1) % TILE_ROWS
    adders = [one_hot((to == at + q * rows) & (at < rows)) for q in range(pieces)]

    def summed(slots):
        flat = slots[...].reshape(packed_rows, wide)
        return jnp.concatenate([dot(adders[q], flat)[:rows] for q in range(pieces)], axis=1)

    tokens = tokens_ref[...].astype(F32)
    xhat, inverse = row_norm(tokens)
    mixed_ref[...] = (tokens + summed(rs_out)).astype(BF16)
    grad = summed(rs_grad)
    grad_mean = jnp.mean(grad, axis=1, keepdims=True)
    projection = jnp.mean(grad * xhat, axis=1, keepdims=True)
    tgrad_ref[...] = (
        cot_ref[...].astype(F32) + inverse * (grad - grad_mean - xhat * projection)
    ).astype(BF16)
    for copy in stores:
        copy.wait()


def body(n_dp, n_mp, tokens, cotangent, up_weight, down_weight):
    rows, width = tokens.shape
    units = up_weight.shape[1]
    feats = width // n_dp
    shard_rows = rows * n_mp
    wide = width * rows // TILE_ROWS
    packed = (n_mp, TILE_ROWS, wide)
    columns = (n_dp, shard_rows, feats)
    hiddens = (n_dp, shard_rows, units)
    in_vmem, anywhere = pl.BlockSpec(memory_space=pltpu.VMEM), pl.BlockSpec(memory_space=pl.ANY)
    exchanged = pl.pallas_call(
        functools.partial(exchange_kernel, n_dp, n_mp),
        out_shape=[
            jax.ShapeDtypeStruct(shape, BF16)
            for shape in (packed, packed, columns, columns, hiddens, hiddens)
        ],
        in_specs=[in_vmem] * 2 + [anywhere] * 2,
        out_specs=[anywhere] * 6,
        scratch_shapes=[
            pltpu.VMEM(up_weight.shape, BF16),
            pltpu.VMEM(down_weight.shape, BF16),
            *[pltpu.VMEM(packed, BF16)] * 4,
            *[pltpu.VMEM(columns, BF16)] * 2,
            *[pltpu.VMEM(hiddens[1:], BF16)] * 2,
            pltpu.VMEM((shard_rows, units), F32),
            *[pltpu.VMEM((shard_rows, width), BF16)] * 2,
            pltpu.SemaphoreType.DMA((2, 4)),
            pltpu.SemaphoreType.DMA((6,)),
            pltpu.SemaphoreType.DMA((4, n_mp)),
            pltpu.SemaphoreType.DMA((4, n_mp)),
            pltpu.SemaphoreType.DMA((4, n_dp)),
            pltpu.SemaphoreType.DMA((4, n_dp)),
        ],
        compiler_params=pltpu.CompilerParams(
            collective_id=0, has_side_effects=True, vmem_limit_bytes=56 * 1024 * 1024
        ),
        cost_estimate=pl.CostEstimate(
            flops=8 * shard_rows * width * units,
            bytes_accessed=4 * width * units,
            transcendentals=2 * shard_rows * units,
        ),
    )(tokens, cotangent, up_weight, down_weight)
    return pl.pallas_call(
        result_kernel,
        out_shape=(
            jax.ShapeDtypeStruct(tokens.shape, BF16),
            jax.ShapeDtypeStruct(tokens.shape, BF16),
            jax.ShapeDtypeStruct((feats, units), BF16),
            jax.ShapeDtypeStruct((units, feats), BF16),
        ),
        in_specs=[in_vmem] * 8,
        out_specs=[in_vmem] * 2 + [anywhere] * 2,
        scratch_shapes=[
            pltpu.VMEM((feats, units), BF16),
            pltpu.VMEM((units, feats), BF16),
            pltpu.SemaphoreType.DMA((2, 8)),
        ],
        compiler_params=pltpu.CompilerParams(vmem_limit_bytes=24 * 1024 * 1024),
        cost_estimate=pl.CostEstimate(
            flops=4 * n_dp * shard_rows * units * feats,
            bytes_accessed=4 * feats * units,
            transcendentals=0,
        ),
    )(tokens, cotangent, *exchanged)


def solution(mesh):
    return jax.shard_map(
        functools.partial(body, mesh.shape["dp"], mesh.shape["mp"]),
        mesh=mesh,
        in_specs=(P(("dp", "mp"), None), P(("dp", "mp"), None), P(None, "mp"), P("mp", None)),
        out_specs=(P(("dp", "mp"), None), P(("dp", "mp"), None), P("dp", "mp"), P("mp", "dp")),
        check_vma=False,
    )
```

time: 41.5 us -> 41 us (0.988)
  local copies, waits for them, and re-layouts: 7.49 us -> 5.7 us
  Pallas kernels: 33 us -> 34.2 us
    unnamed x6 -> x16, local copies, waits for them, and re-layouts: 7.49 us -> 5.7 us
    pallas_call x1 -> x2, Pallas kernels: 33 us -> 34.2 us  [the longest x1 30.8 us: body(): pl.pallas_call(functools.partial(exchange_kernel, n_dp, n_mp), out_shape=...]
where the time goes in v2:
time: 41 us; the launch traced here: 40.6 us
  Pallas kernels  34.2 us (83%)
  local copies, waits for them, and re-layouts  5.7 us (14%)
  between operations  0.68 us (2%)
    pallas_call x1, Pallas kernels, body(): pl.pallas_call(functools.partial(exchange_kernel, n_dp, n_mp), out_shape=...  30.8 us
    unnamed x16, local copies, waits for them, and re-layouts  5.7 us
    pallas_call x1, Pallas kernels, body(): pl.pallas_call(result_kernel, out_shape=(jax.ShapeDtypeStruct(tokens.shap...  3.39 us

profile of v2, /device:TPU:0, one launch (start us, length us, event | category | flops | bytes accessed | tf_op | source)
XLA Modules:
  0.0 40.6 jit_solution(16010641774999223975)
XLA Ops:
  0.6 0.0 copy-start.1
  0.6 0.0 copy-start
  0.7 30.8 %shard_map.75 = (bf16[8,16,768]{2,1,0:T(8,128)(2,1)}, bf16[8,16,768]{2,1,0:T(8,128)(2,1)}, bf16[4,32,768]{2,1,0:T(8,128)(2,1)}, bf16[4,32,768]{2,1,0:T(8,128)(2,...) custom-call(bf16[4,3072]{1,0:T(4,128)(2,1)} %tokens_ref.3, bf16[4,3072]{1,0:T(4,128)(2,1)} %cot_ref.3, ...), custom_call_target="tpu_custom_call" | custom-call | flops 1207959552 | bytes 18874368 | tf_op jit(solution)/shard_map/pallas_call | solution.py:274
  31.5 0.0 copy-done.1
  31.5 0.0 copy-done
  31.5 0.0 copy-start.2
  31.5 1.0 %copy-done.2 = bf16[4,32,1536]{2,1,0:T(8,128)(2,1)S(1)} copy-done((bf16[4,32,1536]{2,1,0:T(8,128)(2,1)S(1)}, bf16[4,32,1536]{2,1,0:T(8,128)(2,1)}, u32[]{:S(2)}) %copy-start.2) | copy-done | bytes 393240
  32.5 0.0 copy-start.3
  32.5 1.0 %copy-done.3 = bf16[4,32,1536]{2,1,0:T(8,128)(2,1)S(1)} copy-done((bf16[4,32,1536]{2,1,0:T(8,128)(2,1)S(1)}, bf16[4,32,1536]{2,1,0:T(8,128)(2,1)}, u32[]{:S(2)}) %copy-start.3) | copy-done | bytes 393240
  33.5 0.0 copy-start.4
  33.5 0.9 %copy-done.4 = bf16[8,16,768]{2,1,0:T(8,128)(2,1)S(1)} copy-done((bf16[8,16,768]{2,1,0:T(8,128)(2,1)S(1)}, bf16[8,16,768]{2,1,0:T(8,128)(2,1)}, u32[]{:S(2)}) %copy-start.4) | copy-done | bytes 196632
  34.4 0.0 copy-start.5
  34.4 0.9 %copy-done.5 = bf16[8,16,768]{2,1,0:T(8,128)(2,1)S(1)} copy-done((bf16[8,16,768]{2,1,0:T(8,128)(2,1)S(1)}, bf16[8,16,768]{2,1,0:T(8,128)(2,1)}, u32[]{:S(2)}) %copy-start.5) | copy-done | bytes 196632
  35.4 0.0 copy-start.6
  35.4 0.9 %copy-done.6 = bf16[4,32,768]{2,1,0:T(8,128)(2,1)S(1)} copy-done((bf16[4,32,768]{2,1,0:T(8,128)(2,1)S(1)}, bf16[4,32,768]{2,1,0:T(8,128)(2,1)}, u32[]{:S(2)}) %copy-start.6) | copy-done | bytes 196632
  36.3 0.0 copy-start.7
  36.3 0.9 %copy-done.7 = bf16[4,32,768]{2,1,0:T(8,128)(2,1)S(1)} copy-done((bf16[4,32,768]{2,1,0:T(8,128)(2,1)S(1)}, bf16[4,32,768]{2,1,0:T(8,128)(2,1)}, u32[]{:S(2)}) %copy-start.7) | copy-done | bytes 196632
  37.2 3.4 %shard_map.76 = (bf16[4,3072]{1,0:T(4,128)(2,1)}, bf16[4,3072]{1,0:T(4,128)(2,1)}, bf16[768,1536]{1,0:T(8,128)(2,1)}, bf16[1536,768]{1,0:T(8,128)(2,1)}) custom-call(bf16[4,3072]{1,0:T(4,128)(2,1)S(1)} %copy-done, bf16[4,3072]{1,0:T(4,128)(2,1)S(1)} %copy-done.1, bf16[8,16,768]{2,1,0:T(8,128)(2,1)S(1)} %copy-done.4, bf16[8,16,768]{2,1,0:T(8,128)(2,1)S(1)} %copy-done.5, ...), custom_call_target="tpu_custom_call" | custom-call | flops 603979776 | bytes 4718592 | tf_op jit(solution)/shard_map/pallas_call | solution.py:306
Async XLA Ops:
  0.6 30.9 %copy-start.1 = (bf16[4,3072]{1,0:T(4,128)(2,1)S(1)}, bf16[4,3072]{1,0:T(4,128)(2,1)}, u32[]{:S(2)}) copy-start(bf16[4,3072]{1,0:T(4,128)(2,1)} %cot_ref.3) | copy-start | bytes 73732
  0.6 30.9 %copy-start = (bf16[4,3072]{1,0:T(4,128)(2,1)S(1)}, bf16[4,3072]{1,0:T(4,128)(2,1)}, u32[]{:S(2)}) copy-start(bf16[4,3072]{1,0:T(4,128)(2,1)} %tokens_ref.3) | copy-start | bytes 73732
  31.5 1.0 %copy-start.2 = (bf16[4,32,1536]{2,1,0:T(8,128)(2,1)S(1)}, bf16[4,32,1536]{2,1,0:T(8,128)(2,1)}, u32[]{:S(2)}) copy-start(bf16[4,32,1536]{2,1,0:T(8,128)(2,1)} %get-tuple-element.14.hid) | copy-start | bytes 1179652
  32.5 1.0 %copy-start.3 = (bf16[4,32,1536]{2,1,0:T(8,128)(2,1)S(1)}, bf16[4,32,1536]{2,1,0:T(8,128)(2,1)}, u32[]{:S(2)}) copy-start(bf16[4,32,1536]{2,1,0:T(8,128)(2,1)} %get-tuple-element.15.act) | copy-start | bytes 1179652
  33.5 0.9 %copy-start.4 = (bf16[8,16,768]{2,1,0:T(8,128)(2,1)S(1)}, bf16[8,16,768]{2,1,0:T(8,128)(2,1)}, u32[]{:S(2)}) copy-start(bf16[8,16,768]{2,1,0:T(8,128)(2,1)} %get-tuple-element.10.rs_out) | copy-start | bytes 589828
  34.4 0.9 %copy-start.5 = (bf16[8,16,768]{2,1,0:T(8,128)(2,1)S(1)}, bf16[8,16,768]{2,1,0:T(8,128)(2,1)}, u32[]{:S(2)}) copy-start(bf16[8,16,768]{2,1,0:T(8,128)(2,1)} %get-tuple-element.11.rs_grad) | copy-start | bytes 589828
  35.4 0.9 %copy-start.6 = (bf16[4,32,768]{2,1,0:T(8,128)(2,1)S(1)}, bf16[4,32,768]{2,1,0:T(8,128)(2,1)}, u32[]{:S(2)}) copy-start(bf16[4,32,768]{2,1,0:T(8,128)(2,1)} %get-tuple-element.12.ncol) | copy-start | bytes 589828
  36.3 0.9 %copy-start.7 = (bf16[4,32,768]{2,1,0:T(8,128)(2,1)S(1)}, bf16[4,32,768]{2,1,0:T(8,128)(2,1)}, u32[]{:S(2)}) copy-start(bf16[4,32,768]{2,1,0:T(8,128)(2,1)} %get-tuple-element.13.ccol) | copy-start | bytes 589828

commit v3 on v2

--- a/solution.py
+++ b/solution.py
@@ -75,13 +75,25 @@
     return centred * inverse, inverse
 
 
+def weight_grad(left, right, out, after=None):
+    n_dp, shard_rows, lefts = left.shape
+    step = chunk_of(lefts)
+    right_rows = right[...].reshape(n_dp * shard_rows, right.shape[2])
+    for i in range(lefts // step):
+        cols = slice(i * step, (i + 1) * step)
+        left_rows = left[:, :, cols].reshape(n_dp * shard_rows, step)
+        out[cols, :] = dot(left_rows, right_rows, 0, 0).astype(BF16)
+        if after is not None:
+            after(i, cols)
+
+
 def exchange_kernel(
     n_dp, n_mp,
     tokens_ref, cot_ref, up_hbm, down_hbm,
-    rs_out, rs_grad, ncol, ccol, hid, act,
+    rs_out, rs_grad, ncol, act, down_out,
     up_v, down_v,
     gather_n, gather_c, rs_out_send, rs_grad_send,
-    ncol_send, ccol_send, hid_own, act_own, slope, rows_n, rows_c,
+    ncol_send, ccol_send, ccol, hid, hid_own, act_own, slope, rows_n, rows_c,
     load_sem, own_sem, mp_send, mp_recv, dp_send, dp_recv,
 ):
     rows, width = tokens_ref.shape
@@ -159,7 +171,7 @@
     for copy in crossed_n:
         copy.wait_recv()
     unpack(gather_n, rows_n)
-    arrivals = send_columns(0, rows_n, ncol_send, ncol)
+    got_ncol = send_columns(0, rows_n, ncol_send, ncol)
 
     for copy in loads[:parts]:
         copy.wait()
@@ -177,7 +189,7 @@
     for copy in crossed_c:
         copy.wait_recv()
     unpack(gather_c, rows_c)
-    arrivals += send_columns(1, rows_c, ccol_send, ccol)
+    got_ccol = send_columns(1, rows_c, ccol_send, ccol)
 
     for copy in loads[parts:]:
         copy.wait()
@@ -191,7 +203,7 @@
         keep(send.at[0], slots, 2 + kind)
         return got
 
-    arrivals += scatter(
+    got_out = scatter(
         2, lambda q: dot(hid_own[...], down_v[:, q * wide:(q + 1) * wide]), rs_out_send, rs_out
     )
     for i in range(units // step):
@@ -200,45 +212,41 @@
         act_own[:, cols] = (hidden_grad * slope[:, cols]).astype(BF16)
     straight_a, crossed_a = dp_spread(3, act_own, act)
     keep(act_own, act, 3)
+    got_grad = scatter(
+        3, lambda q: dot(act_own[...], up_v[q * wide:(q + 1) * wide, :], 1, 1), rs_grad_send, rs_grad
+    )
     dp_pass_on(2, hid, straight_h, crossed_h)
-    arrivals += scatter(
-        3, lambda q: dot(act_own[...], up_v[q * wide:(q + 1) * wide, :], 1, 1), rs_grad_send, rs_grad
-    )
-    dp_pass_on(3, act, straight_a, crossed_a)
-
-    for copy in arrivals + crossed_h + crossed_a:
+    for copy in got_ccol + crossed_h:
         copy.wait_recv()
     for copy in own:
         copy.wait()
+    weight_grad(hid, ccol, down_out)
+    dp_pass_on(3, act, straight_a, crossed_a)
+
+    for copy in got_ncol + got_out + got_grad + crossed_a:
+        copy.wait_recv()
     for copy in sent:
         copy.wait_send()
 
 
 def result_kernel(
-    tokens_ref, cot_ref, rs_out, rs_grad, ncol, ccol, hid, act,
+    tokens_ref, cot_ref, rs_out, rs_grad, ncol, act, down_out,
     mixed_ref, tgrad_ref, up_grad_hbm, down_grad_hbm,
-    up_out, down_out, out_sem,
+    up_out, down_sem, up_sem,
 ):
     rows, width = tokens_ref.shape
     pieces = TILE_ROWS // rows
     n_mp, _, wide = rs_out.shape
     packed_rows = TILE_ROWS * n_mp
-    stores = []
-
-    def weight_grad(left, right, out, out_hbm, which):
-        n_dp, shard_rows, lefts = left.shape
-        step = chunk_of(lefts)
-        right_rows = right[...].reshape(n_dp * shard_rows, right.shape[2])
-        for i in range(lefts // step):
-            cols = slice(i * step, (i + 1) * step)
-            left_rows = left[:, :, cols].reshape(n_dp * shard_rows, step)
-            out[cols, :] = dot(left_rows, right_rows, 0, 0).astype(BF16)
-            copy = pltpu.make_async_copy(out.at[cols], out_hbm.at[cols], out_sem.at[which, i])
-            copy.start()
-            stores.append(copy)
-
-    weight_grad(hid, ccol, down_out, down_grad_hbm, 0)
-    weight_grad(ncol, act, up_out, up_grad_hbm, 1)
+    stores = [pltpu.make_async_copy(down_out, down_grad_hbm, down_sem)]
+    stores[0].start()
+
+    def store_up(i, cols):
+        copy = pltpu.make_async_copy(up_out.at[cols], up_grad_hbm.at[cols], up_sem.at[i])
+        copy.start()
+        stores.append(copy)
+
+    weight_grad(ncol, act, up_out, store_up)
 
     at = lax.broadcasted_iota(jnp.int32, (8, packed_rows), 0)
     to = lax.broadcasted_iota(jnp.int32, (8, packed_rows), 1) % TILE_ROWS
@@ -274,16 +282,17 @@
     exchanged = pl.pallas_call(
         functools.partial(exchange_kernel, n_dp, n_mp),
         out_shape=[
-            jax.ShapeDtypeStruct(shape, BF16)
-            for shape in (packed, packed, columns, columns, hiddens, hiddens)
+            pltpu.VMEM(shape, BF16)
+            for shape in (packed, packed, columns, hiddens, (units, feats))
         ],
         in_specs=[in_vmem] * 2 + [anywhere] * 2,
-        out_specs=[anywhere] * 6,
+        out_specs=[in_vmem] * 5,
         scratch_shapes=[
             pltpu.VMEM(up_weight.shape, BF16),
             pltpu.VMEM(down_weight.shape, BF16),
             *[pltpu.VMEM(packed, BF16)] * 4,
-            *[pltpu.VMEM(columns, BF16)] * 2,
+            *[pltpu.VMEM(columns, BF16)] * 3,
+            pltpu.VMEM(hiddens, BF16),
             *[pltpu.VMEM(hiddens[1:], BF16)] * 2,
             pltpu.VMEM((shard_rows, units), F32),
             *[pltpu.VMEM((shard_rows, width), BF16)] * 2,
@@ -311,12 +320,12 @@
             jax.ShapeDtypeStruct((feats, units), BF16),
             jax.ShapeDtypeStruct((units, feats), BF16),
         ),
-        in_specs=[in_vmem] * 8,
+        in_specs=[in_vmem] * 7,
         out_specs=[in_vmem] * 2 + [anywhere] * 2,
         scratch_shapes=[
             pltpu.VMEM((feats, units), BF16),
-            pltpu.VMEM((units, feats), BF16),
-            pltpu.SemaphoreType.DMA((2, 8)),
+            pltpu.SemaphoreType.DMA,
+            pltpu.SemaphoreType.DMA((8,)),
         ],
         compiler_params=pltpu.CompilerParams(vmem_limit_bytes=24 * 1024 * 1024),
         cost_estimate=pl.CostEstimate(

time: 41 us -> 35 us (0.85)
  local copies, waits for them, and re-layouts: 5.7 us -> 0.01 us
    unnamed x16 -> x4, local copies, waits for them, and re-layouts: 5.7 us -> 0.01 us
    pallas_call x1, Pallas kernels: 3.39 us -> 2.95 us  [body(): pl.pallas_call(result_kernel, out_shape=(jax.ShapeDtypeStruct(tokens.shap...]
where the time goes in v3:
time: 35 us; the launch traced here: 34.8 us
  Pallas kernels  34.1 us (97%)
  between operations  0.67 us (2%)
    pallas_call x1, Pallas kernels, body(): pl.pallas_call(functools.partial(exchange_kernel, n_dp, n_mp), out_shape=...  31.2 us
    pallas_call x1, Pallas kernels, body(): pl.pallas_call(result_kernel, out_shape=(jax.ShapeDtypeStruct(tokens.shap...  2.95 us

profile of v3, /device:TPU:0, one launch (start us, length us, event | category | flops | bytes accessed | tf_op | source)
XLA Modules:
  0.0 34.8 jit_solution(18170683745766430223)
XLA Ops:
  0.6 0.0 copy-start.1
  0.6 0.0 copy-start
  0.7 31.2 %shard_map.75 = (bf16[8,16,768]{2,1,0:T(8,128)(2,1)S(1)}, bf16[8,16,768]{2,1,0:T(8,128)(2,1)S(1)}, bf16[4,32,768]{2,1,0:T(8,128)(2,1)S(1)}, bf16[4,32,1536]{2,1,0:T(8,128)(2,1)S(1)}, bf16[1536,768]{1,0:T(8,128)(2,1)S(1)}) custom-call(bf16[4,3072]{1,0:T(4,128)(2,1)} %tokens_ref.3, bf16[4,3072]{1,0:T(4,128)(2,1)} %cot_ref.3, bf16[3072,1536]{1,0:T(8,128)(2,1)} %up_hbm.1, ...), custom_call_target="tpu_custom_call" | custom-call | flops 1207959552 | bytes 18874368 | tf_op jit(solution)/shard_map/pallas_call | solution.py:282
  31.8 0.0 copy-done.1
  31.8 0.0 copy-done
  31.8 3.0 %shard_map.76 = (bf16[4,3072]{1,0:T(4,128)(2,1)}, bf16[4,3072]{1,0:T(4,128)(2,1)}, bf16[768,1536]{1,0:T(8,128)(2,1)}, bf16[1536,768]{1,0:T(8,128)(2,1)}) custom-call(bf16[4,3072]{1,0:T(4,128)(2,1)S(1)} %copy-done, bf16[4,3072]{1,0:T(4,128)(2,1)S(1)} %copy-done.1, bf16[8,16,768]{2,1,0:T(8,128)(2,1)S(1)} %get-tuple-element.9.rs_out, ...), custom_call_target="tpu_custom_call" | custom-call | flops 603979776 | bytes 4718592 | tf_op jit(solution)/shard_map/pallas_call | solution.py:315
Async XLA Ops:
  0.6 31.2 %copy-start.1 = (bf16[4,3072]{1,0:T(4,128)(2,1)S(1)}, bf16[4,3072]{1,0:T(4,128)(2,1)}, u32[]{:S(2)}) copy-start(bf16[4,3072]{1,0:T(4,128)(2,1)} %cot_ref.3) | copy-start | bytes 73732
  0.6 31.2 %copy-start = (bf16[4,3072]{1,0:T(4,128)(2,1)S(1)}, bf16[4,3072]{1,0:T(4,128)(2,1)}, u32[]{:S(2)}) copy-start(bf16[4,3072]{1,0:T(4,128)(2,1)} %tokens_ref.3) | copy-start | bytes 73732

commit v4 on v3

--- a/solution.py
+++ b/solution.py
@@ -10,6 +10,7 @@
 ROOT_HALF = 0.7071067811865476
 DENSITY_SCALE = 0.3989422804014327
 TILE_ROWS = 16
+HALVES = 2
 MESH = pl.DeviceIdType.MESH
 F32 = jnp.float32
 BF16 = jnp.bfloat16
@@ -75,7 +76,7 @@
     return centred * inverse, inverse
 
 
-def weight_grad(left, right, out, after=None):
+def weight_grad(left, right, out):
     n_dp, shard_rows, lefts = left.shape
     step = chunk_of(lefts)
     right_rows = right[...].reshape(n_dp * shard_rows, right.shape[2])
@@ -83,17 +84,15 @@
         cols = slice(i * step, (i + 1) * step)
         left_rows = left[:, :, cols].reshape(n_dp * shard_rows, step)
         out[cols, :] = dot(left_rows, right_rows, 0, 0).astype(BF16)
-        if after is not None:
-            after(i, cols)
 
 
 def exchange_kernel(
     n_dp, n_mp,
     tokens_ref, cot_ref, up_hbm, down_hbm,
-    rs_out, rs_grad, ncol, act, down_out,
+    rs_out, rs_grad, down_out, up_out,
     up_v, down_v,
     gather_n, gather_c, rs_out_send, rs_grad_send,
-    ncol_send, ccol_send, ccol, hid, hid_own, act_own, slope, rows_n, rows_c,
+    ncol_send, ccol_send, ncol, ccol, hid, act, hid_own, act_own, slope, rows_n, rows_c,
     load_sem, own_sem, mp_send, mp_recv, dp_send, dp_recv,
 ):
     rows, width = tokens_ref.shape
@@ -194,18 +193,23 @@
     for copy in loads[parts:]:
         copy.wait()
 
+    half = wide // HALVES
+
     def scatter(kind, partial_of, send, slots):
-        total = jnp.zeros((packed_rows, wide), F32)
-        for q in range(pieces):
-            total += dot(unpackers[q], partial_of(q).astype(BF16), 0, 0)
-        send[...] = total.astype(BF16).reshape(n_mp, TILE_ROWS, wide)
-        got = [mp_start(kind, send.at[mp_opposite(b)], slots.at[b], b) for b in range(1, n_mp)]
-        keep(send.at[0], slots, 2 + kind)
+        got = []
+        for h in range(HALVES):
+            partial = partial_of(slice(h * pieces * half, (h + 1) * pieces * half)).astype(BF16)
+            total = jnp.zeros((packed_rows, half), F32)
+            for q in range(pieces):
+                total += dot(unpackers[q], partial[:, q * half:(q + 1) * half], 0, 0)
+            send[h] = total.astype(BF16).reshape(n_mp, TILE_ROWS, half)
+            got += [
+                mp_start(kind + h, send.at[h, mp_opposite(b)], slots.at[h, b], b)
+                for b in range(1, n_mp)
+            ]
+            keep(send.at[h, 0], slots.at[h], 2 + kind + h)
         return got
 
-    got_out = scatter(
-        2, lambda q: dot(hid_own[...], down_v[:, q * wide:(q + 1) * wide]), rs_out_send, rs_out
-    )
     for i in range(units // step):
         cols = slice(i * step, (i + 1) * step)
         hidden_grad = dot(rows_c[...], down_v[cols, :], 1, 1)
@@ -213,48 +217,50 @@
     straight_a, crossed_a = dp_spread(3, act_own, act)
     keep(act_own, act, 3)
     got_grad = scatter(
-        3, lambda q: dot(act_own[...], up_v[q * wide:(q + 1) * wide, :], 1, 1), rs_grad_send, rs_grad
+        2 + HALVES, lambda cols: dot(act_own[...], up_v[cols, :], 1, 1), rs_grad_send, rs_grad
     )
     dp_pass_on(2, hid, straight_h, crossed_h)
+    got_out = scatter(2, lambda cols: dot(hid_own[...], down_v[:, cols]), rs_out_send, rs_out)
+    dp_pass_on(3, act, straight_a, crossed_a)
     for copy in got_ccol + crossed_h:
         copy.wait_recv()
     for copy in own:
         copy.wait()
     weight_grad(hid, ccol, down_out)
-    dp_pass_on(3, act, straight_a, crossed_a)
-
-    for copy in got_ncol + got_out + got_grad + crossed_a:
+    for copy in got_ncol + crossed_a:
+        copy.wait_recv()
+    weight_grad(ncol, act, up_out)
+    for copy in got_grad + got_out:
         copy.wait_recv()
     for copy in sent:
         copy.wait_send()
 
 
 def result_kernel(
-    tokens_ref, cot_ref, rs_out, rs_grad, ncol, act, down_out,
+    tokens_ref, cot_ref, rs_out, rs_grad, down_out, up_out,
     mixed_ref, tgrad_ref, up_grad_hbm, down_grad_hbm,
-    up_out, down_sem, up_sem,
+    store_sem,
 ):
     rows, width = tokens_ref.shape
     pieces = TILE_ROWS // rows
-    n_mp, _, wide = rs_out.shape
+    _, n_mp, _, half = rs_out.shape
     packed_rows = TILE_ROWS * n_mp
-    stores = [pltpu.make_async_copy(down_out, down_grad_hbm, down_sem)]
-    stores[0].start()
-
-    def store_up(i, cols):
-        copy = pltpu.make_async_copy(up_out.at[cols], up_grad_hbm.at[cols], up_sem.at[i])
+    stores = [
+        pltpu.make_async_copy(down_out, down_grad_hbm, store_sem.at[0]),
+        pltpu.make_async_copy(up_out, up_grad_hbm, store_sem.at[1]),
+    ]
+    for copy in stores:
         copy.start()
-        stores.append(copy)
-
-    weight_grad(ncol, act, up_out, store_up)
 
     at = lax.broadcasted_iota(jnp.int32, (8, packed_rows), 0)
     to = lax.broadcasted_iota(jnp.int32, (8, packed_rows), 1) % TILE_ROWS
     adders = [one_hot((to == at + q * rows) & (at < rows)) for q in range(pieces)]
 
     def summed(slots):
-        flat = slots[...].reshape(packed_rows, wide)
-        return jnp.concatenate([dot(adders[q], flat)[:rows] for q in range(pieces)], axis=1)
+        flats = [slots[h].reshape(packed_rows, half) for h in range(HALVES)]
+        return jnp.concatenate(
+            [dot(adders[q], flat)[:rows] for flat in flats for q in range(pieces)], axis=1
+        )
 
     tokens = tokens_ref[...].astype(F32)
     xhat, inverse = row_norm(tokens)
@@ -276,6 +282,7 @@
     shard_rows = rows * n_mp
     wide = width * rows // TILE_ROWS
     packed = (n_mp, TILE_ROWS, wide)
+    scattered = (HALVES, n_mp, TILE_ROWS, wide // HALVES)
     columns = (n_dp, shard_rows, feats)
     hiddens = (n_dp, shard_rows, units)
     in_vmem, anywhere = pl.BlockSpec(memory_space=pltpu.VMEM), pl.BlockSpec(memory_space=pl.ANY)
@@ -283,23 +290,24 @@
         functools.partial(exchange_kernel, n_dp, n_mp),
         out_shape=[
             pltpu.VMEM(shape, BF16)
-            for shape in (packed, packed, columns, hiddens, (units, feats))
+            for shape in (scattered, scattered, (units, feats), (feats, units))
         ],
         in_specs=[in_vmem] * 2 + [anywhere] * 2,
-        out_specs=[in_vmem] * 5,
+        out_specs=[in_vmem] * 4,
         scratch_shapes=[
             pltpu.VMEM(up_weight.shape, BF16),
             pltpu.VMEM(down_weight.shape, BF16),
-            *[pltpu.VMEM(packed, BF16)] * 4,
-            *[pltpu.VMEM(columns, BF16)] * 3,
-            pltpu.VMEM(hiddens, BF16),
+            *[pltpu.VMEM(packed, BF16)] * 2,
+            *[pltpu.VMEM(scattered, BF16)] * 2,
+            *[pltpu.VMEM(columns, BF16)] * 4,
+            *[pltpu.VMEM(hiddens, BF16)] * 2,
             *[pltpu.VMEM(hiddens[1:], BF16)] * 2,
             pltpu.VMEM((shard_rows, units), F32),
             *[pltpu.VMEM((shard_rows, width), BF16)] * 2,
             pltpu.SemaphoreType.DMA((2, 4)),
-            pltpu.SemaphoreType.DMA((6,)),
-            pltpu.SemaphoreType.DMA((4, n_mp)),
-            pltpu.SemaphoreType.DMA((4, n_mp)),
+            pltpu.SemaphoreType.DMA((4 + 2 * HALVES,)),
+            pltpu.SemaphoreType.DMA((2 + 2 * HALVES, n_mp)),
+            pltpu.SemaphoreType.DMA((2 + 2 * HALVES, n_mp)),
             pltpu.SemaphoreType.DMA((4, n_dp)),
             pltpu.SemaphoreType.DMA((4, n_dp)),
         ],
@@ -320,16 +328,12 @@
             jax.ShapeDtypeStruct((feats, units), BF16),
             jax.ShapeDtypeStruct((units, feats), BF16),
         ),
-        in_specs=[in_vmem] * 7,
+        in_specs=[in_vmem] * 6,
         out_specs=[in_vmem] * 2 + [anywhere] * 2,
-        scratch_shapes=[
-            pltpu.VMEM((feats, units), BF16),
-            pltpu.SemaphoreType.DMA,
-            pltpu.SemaphoreType.DMA((8,)),
-        ],
+        scratch_shapes=[pltpu.SemaphoreType.DMA((2,))],
         compiler_params=pltpu.CompilerParams(vmem_limit_bytes=24 * 1024 * 1024),
         cost_estimate=pl.CostEstimate(
-            flops=4 * n_dp * shard_rows * units * feats,
+            flops=0,
             bytes_accessed=4 * feats * units,
             transcendentals=0,
         ),

time: 35 us -> 35.8 us (1.023)
  Pallas kernels: 34.1 us -> 35 us
    pallas_call x1, Pallas kernels: 31.2 us -> 32.1 us  [body(): pl.pallas_call(functools.partial(exchange_kernel, n_dp, n_mp), out_shape=...]
where the time goes in v4:
time: 35.8 us; the launch traced here: 35.6 us
  Pallas kernels  35 us (98%)
  between operations  0.67 us (2%)
    pallas_call x1, Pallas kernels, body(): pl.pallas_call(functools.partial(exchange_kernel, n_dp, n_mp), out_shape=...  32.1 us
    pallas_call x1, Pallas kernels, body(): pl.pallas_call(result_kernel, out_shape=(jax.ShapeDtypeStruct(tokens.shap...  2.85 us

profile of v4, /device:TPU:0, one launch (start us, length us, event | category | flops | bytes accessed | tf_op | source)
XLA Modules:
  0.0 35.6 jit_solution(16027802827134953036)
XLA Ops:
  0.6 0.0 copy-start.1
  0.6 0.0 copy-start
  0.7 32.1 %shard_map.75 = (bf16[2,8,16,384]{3,2,1,0:T(8,128)(2,1)S(1)}, bf16[2,8,16,384]{3,2,1,0:T(8,128)(2,1)S(1)}, bf16[1536,768]{1,0:T(8,128)(2,1)S(1)}, bf16[768,1536]{1,0:T(8,128)(2,1)S(1)}) custom-call(bf16[4,3072]{1,0:T(4,128)(2,1)} %tokens_ref.3, bf16[4,3072]{1,0:T(4,128)(2,1)} %cot_ref.3, bf16[3072,1536]{1,0:T(8,128)(2,1)} %up_hbm.1, bf16[1536,3072]{1,0:T(8,128)(2,1)} %down_hbm.1), custom_call_target="tpu_custom_call" | custom-call | flops 1207959552 | bytes 18874368 | tf_op jit(solution)/shard_map/pallas_call | solution.py:289
  32.8 0.0 copy-done.1
  32.8 0.0 copy-done
  32.8 2.9 %shard_map.76 = (bf16[4,3072]{1,0:T(4,128)(2,1)}, bf16[4,3072]{1,0:T(4,128)(2,1)}, bf16[768,1536]{1,0:T(8,128)(2,1)}, bf16[1536,768]{1,0:T(8,128)(2,1)}) custom-call(bf16[4,3072]{1,0:T(4,128)(2,1)S(1)} %copy-done, bf16[4,3072]{1,0:T(4,128)(2,1)S(1)} %copy-done.1, bf16[2,8,16,384]{3,2,1,0:T(8,128)(2,1)S(1)} %get-tuple-element.8.rs_out, ...), custom_call_target="tpu_custom_call" | custom-call | bytes 4718592 | tf_op jit(solution)/shard_map/pallas_call | solution.py:323
Async XLA Ops:
  0.6 32.1 %copy-start.1 = (bf16[4,3072]{1,0:T(4,128)(2,1)S(1)}, bf16[4,3072]{1,0:T(4,128)(2,1)}, u32[]{:S(2)}) copy-start(bf16[4,3072]{1,0:T(4,128)(2,1)} %cot_ref.3) | copy-start | bytes 73732
  0.6 32.1 %copy-start = (bf16[4,3072]{1,0:T(4,128)(2,1)S(1)}, bf16[4,3072]{1,0:T(4,128)(2,1)}, u32[]{:S(2)}) copy-start(bf16[4,3072]{1,0:T(4,128)(2,1)} %tokens_ref.3) | copy-start | bytes 73732

commit v5 on v4

--- a/solution.py
+++ b/solution.py
@@ -10,7 +10,7 @@
 ROOT_HALF = 0.7071067811865476
 DENSITY_SCALE = 0.3989422804014327
 TILE_ROWS = 16
-HALVES = 2
+HALVES = 1
 MESH = pl.DeviceIdType.MESH
 F32 = jnp.float32
 BF16 = jnp.bfloat16
@@ -76,7 +76,7 @@
     return centred * inverse, inverse
 
 
-def weight_grad(left, right, out):
+def weight_grad(left, right, out, after=None):
     n_dp, shard_rows, lefts = left.shape
     step = chunk_of(lefts)
     right_rows = right[...].reshape(n_dp * shard_rows, right.shape[2])
@@ -84,15 +84,17 @@
         cols = slice(i * step, (i + 1) * step)
         left_rows = left[:, :, cols].reshape(n_dp * shard_rows, step)
         out[cols, :] = dot(left_rows, right_rows, 0, 0).astype(BF16)
+        if after is not None:
+            after(i, cols)
 
 
 def exchange_kernel(
     n_dp, n_mp,
     tokens_ref, cot_ref, up_hbm, down_hbm,
-    rs_out, rs_grad, down_out, up_out,
+    rs_out, rs_grad, ncol, act, down_out,
     up_v, down_v,
     gather_n, gather_c, rs_out_send, rs_grad_send,
-    ncol_send, ccol_send, ncol, ccol, hid, act, hid_own, act_own, slope, rows_n, rows_c,
+    ncol_send, ccol_send, ccol, hid, hid_own, act_own, slope, rows_n, rows_c,
     load_sem, own_sem, mp_send, mp_recv, dp_send, dp_recv,
 ):
     rows, width = tokens_ref.shape
@@ -139,15 +141,19 @@
     straight_n, crossed_n = mp_spread(0, gather_n.at[0], gather_n)
     straight_c, crossed_c = mp_spread(1, gather_c.at[0], gather_c)
 
-    at = lax.broadcasted_iota(jnp.int32, (shard_rows, packed_rows), 0)
-    to = lax.broadcasted_iota(jnp.int32, (shard_rows, packed_rows), 1)
-    home = at + (at // rows) * (TILE_ROWS - rows)
-    unpackers = [one_hot(to == home + q * rows) for q in range(pieces)]
+    def home(packed):
+        return packed % TILE_ROWS // rows * shard_rows + packed // TILE_ROWS * rows + packed % rows
+
+    square = (packed_rows, packed_rows)
+    first = lax.broadcasted_iota(jnp.int32, square, 0)
+    second = lax.broadcasted_iota(jnp.int32, square, 1)
+    packer = one_hot(second == home(first))
+    unpacker = one_hot(first == home(second))
 
     def unpack(gathered, out):
-        flat = gathered[...].reshape(packed_rows, wide)
+        flat = dot(unpacker, gathered[...].reshape(packed_rows, wide)).astype(BF16)
         for q in range(pieces):
-            out[:, q * wide:(q + 1) * wide] = dot(unpackers[q], flat).astype(BF16)
+            out[:, q * wide:(q + 1) * wide] = flat[q * shard_rows:(q + 1) * shard_rows]
 
     own = []
 
@@ -199,9 +205,10 @@
         got = []
         for h in range(HALVES):
             partial = partial_of(slice(h * pieces * half, (h + 1) * pieces * half)).astype(BF16)
-            total = jnp.zeros((packed_rows, half), F32)
-            for q in range(pieces):
-                total += dot(unpackers[q], partial[:, q * half:(q + 1) * half], 0, 0)
+            stacked = jnp.concatenate(
+                [partial[:, q * half:(q + 1) * half] for q in range(pieces)], axis=0
+            )
+            total = dot(packer, stacked)
             send[h] = total.astype(BF16).reshape(n_mp, TILE_ROWS, half)
             got += [
                 mp_start(kind + h, send.at[h, mp_opposite(b)], slots.at[h, b], b)
@@ -229,7 +236,6 @@
     weight_grad(hid, ccol, down_out)
     for copy in got_ncol + crossed_a:
         copy.wait_recv()
-    weight_grad(ncol, act, up_out)
     for copy in got_grad + got_out:
         copy.wait_recv()
     for copy in sent:
@@ -237,20 +243,26 @@
 
 
 def result_kernel(
-    tokens_ref, cot_ref, rs_out, rs_grad, down_out, up_out,
+    tokens_ref, cot_ref, rs_out, rs_grad, ncol, act, down_out,
     mixed_ref, tgrad_ref, up_grad_hbm, down_grad_hbm,
-    store_sem,
+    up_out, down_sem, up_sem,
 ):
     rows, width = tokens_ref.shape
     pieces = TILE_ROWS // rows
     _, n_mp, _, half = rs_out.shape
     packed_rows = TILE_ROWS * n_mp
-    stores = [
-        pltpu.make_async_copy(down_out, down_grad_hbm, store_sem.at[0]),
-        pltpu.make_async_copy(up_out, up_grad_hbm, store_sem.at[1]),
-    ]
-    for copy in stores:
+    stores = []
+
+    def store(out, out_hbm, cols, sem):
+        copy = pltpu.make_async_copy(out.at[cols], out_hbm.at[cols], sem)
         copy.start()
+        stores.append(copy)
+
+    parts = down_sem.shape[0]
+    step = down_out.shape[0] // parts
+    for i in range(parts):
+        store(down_out, down_grad_hbm, slice(i * step, (i + 1) * step), down_sem.at[i])
+    weight_grad(ncol, act, up_out, lambda i, cols: store(up_out, up_grad_hbm, cols, up_sem.at[i]))
 
     at = lax.broadcasted_iota(jnp.int32, (8, packed_rows), 0)
     to = lax.broadcasted_iota(jnp.int32, (8, packed_rows), 1) % TILE_ROWS
@@ -290,17 +302,17 @@
         functools.partial(exchange_kernel, n_dp, n_mp),
         out_shape=[
             pltpu.VMEM(shape, BF16)
-            for shape in (scattered, scattered, (units, feats), (feats, units))
+            for shape in (scattered, scattered, columns, hiddens, (units, feats))
         ],
         in_specs=[in_vmem] * 2 + [anywhere] * 2,
-        out_specs=[in_vmem] * 4,
+        out_specs=[in_vmem] * 5,
         scratch_shapes=[
             pltpu.VMEM(up_weight.shape, BF16),
             pltpu.VMEM(down_weight.shape, BF16),
             *[pltpu.VMEM(packed, BF16)] * 2,
             *[pltpu.VMEM(scattered, BF16)] * 2,
-            *[pltpu.VMEM(columns, BF16)] * 4,
-            *[pltpu.VMEM(hiddens, BF16)] * 2,
+            *[pltpu.VMEM(columns, BF16)] * 3,
+            pltpu.VMEM(hiddens, BF16),
             *[pltpu.VMEM(hiddens[1:], BF16)] * 2,
             pltpu.VMEM((shard_rows, units), F32),
             *[pltpu.VMEM((shard_rows, width), BF16)] * 2,
@@ -328,12 +340,16 @@
             jax.ShapeDtypeStruct((feats, units), BF16),
             jax.ShapeDtypeStruct((units, feats), BF16),
         ),
-        in_specs=[in_vmem] * 6,
+        in_specs=[in_vmem] * 7,
         out_specs=[in_vmem] * 2 + [anywhere] * 2,
-        scratch_shapes=[pltpu.SemaphoreType.DMA((2,))],
+        scratch_shapes=[
+            pltpu.VMEM((feats, units), BF16),
+            pltpu.SemaphoreType.DMA((4,)),
+            pltpu.SemaphoreType.DMA((8,)),
+        ],
         compiler_params=pltpu.CompilerParams(vmem_limit_bytes=24 * 1024 * 1024),
         cost_estimate=pl.CostEstimate(
-            flops=0,
+            flops=2 * n_dp * shard_rows * units * feats,
             bytes_accessed=4 * feats * units,
             transcendentals=0,
         ),

time: 35.8 us -> 35.6 us (level)
    pallas_call x1, Pallas kernels: 32.1 us -> 31.7 us  [body(): pl.pallas_call(functools.partial(exchange_kernel, n_dp, n_mp), out_shape=...]
where the time goes in v5:
time: 35.6 us; the launch traced here: 35.4 us
  Pallas kernels  34.7 us (97%)
  between operations  0.67 us (2%)
    pallas_call x1, Pallas kernels, body(): pl.pallas_call(functools.partial(exchange_kernel, n_dp, n_mp), out_shape=...  31.7 us
    pallas_call x1, Pallas kernels, body(): pl.pallas_call(result_kernel, out_shape=(jax.ShapeDtypeStruct(tokens.shap...  2.98 us

profile of v5, /device:TPU:0, one launch (start us, length us, event | category | flops | bytes accessed | tf_op | source)
XLA Modules:
  0.0 35.4 jit_solution(2438000829743194569)
XLA Ops:
  0.6 0.0 copy-start.1
  0.6 0.0 copy-start
  0.7 31.7 %shard_map.75 = (bf16[1,8,16,768]{3,2,1,0:T(8,128)(2,1)S(1)}, bf16[1,8,16,768]{3,2,1,0:T(8,128)(2,1)S(1)}, bf16[4,32,768]{2,1,0:T(8,128)(2,1)S(1)}, bf16[4,32,15...) custom-call(bf16[4,3072]{1,0:T(4,128)(2,1)} %tokens_ref.3, bf16[4,3072]{1,0:T(4,128)(2,1)} %cot_ref.3, ...), custom_call_target="tpu_custom_call" | custom-call | flops 1207959552 | bytes 18874368 | tf_op jit(solution)/shard_map/pallas_call | solution.py:301
  32.4 0.0 copy-done.1
  32.4 0.0 copy-done
  32.4 3.0 %shard_map.76 = (bf16[4,3072]{1,0:T(4,128)(2,1)}, bf16[4,3072]{1,0:T(4,128)(2,1)}, bf16[768,1536]{1,0:T(8,128)(2,1)}, bf16[1536,768]{1,0:T(8,128)(2,1)}) custom-call(bf16[4,3072]{1,0:T(4,128)(2,1)S(1)} %copy-done, bf16[4,3072]{1,0:T(4,128)(2,1)S(1)} %copy-done.1, bf16[1,8,16,768]{3,2,1,0:T(8,128)(2,1)S(1)} %get-tuple-element.9.rs_out, ...), custom_call_target="tpu_custom_call" | custom-call | flops 301989888 | bytes 4718592 | tf_op jit(solution)/shard_map/pallas_call | solution.py:335
Async XLA Ops:
  0.6 31.8 %copy-start.1 = (bf16[4,3072]{1,0:T(4,128)(2,1)S(1)}, bf16[4,3072]{1,0:T(4,128)(2,1)}, u32[]{:S(2)}) copy-start(bf16[4,3072]{1,0:T(4,128)(2,1)} %cot_ref.3) | copy-start | bytes 73732
  0.6 31.8 %copy-start = (bf16[4,3072]{1,0:T(4,128)(2,1)S(1)}, bf16[4,3072]{1,0:T(4,128)(2,1)}, u32[]{:S(2)}) copy-start(bf16[4,3072]{1,0:T(4,128)(2,1)} %tokens_ref.3) | copy-start | bytes 73732

commit v6 on v5

--- a/solution.py
+++ b/solution.py
@@ -217,6 +217,7 @@
             keep(send.at[h, 0], slots.at[h], 2 + kind + h)
         return got
 
+    got_out = scatter(2, lambda cols: dot(hid_own[...], down_v[:, cols]), rs_out_send, rs_out)
     for i in range(units // step):
         cols = slice(i * step, (i + 1) * step)
         hidden_grad = dot(rows_c[...], down_v[cols, :], 1, 1)
@@ -227,7 +228,6 @@
         2 + HALVES, lambda cols: dot(act_own[...], up_v[cols, :], 1, 1), rs_grad_send, rs_grad
     )
     dp_pass_on(2, hid, straight_h, crossed_h)
-    got_out = scatter(2, lambda cols: dot(hid_own[...], down_v[:, cols]), rs_out_send, rs_out)
     dp_pass_on(3, act, straight_a, crossed_a)
     for copy in got_ccol + crossed_h:
         copy.wait_recv()

time: 35.6 us -> 34.3 us (0.963)
  Pallas kernels: 34.7 us -> 33.4 us
    pallas_call x1, Pallas kernels: 31.7 us -> 30.4 us  [body(): pl.pallas_call(functools.partial(exchange_kernel, n_dp, n_mp), out_shape=...]
where the time goes in v6:
time: 34.3 us; the launch traced here: 34.1 us
  Pallas kernels  33.4 us (97%)
  between operations  0.67 us (2%)
    pallas_call x1, Pallas kernels, body(): pl.pallas_call(functools.partial(exchange_kernel, n_dp, n_mp), out_shape=...  30.4 us
    pallas_call x1, Pallas kernels, body(): pl.pallas_call(result_kernel, out_shape=(jax.ShapeDtypeStruct(tokens.shap...  2.98 us

profile of v6, /device:TPU:0, one launch (start us, length us, event | category | flops | bytes accessed | tf_op | source)
XLA Modules:
  0.0 34.1 jit_solution(7499536505781512785)
XLA Ops:
  0.6 0.0 copy-start.1
  0.6 0.0 copy-start
  0.7 30.4 %shard_map.75 = (bf16[1,8,16,768]{3,2,1,0:T(8,128)(2,1)S(1)}, bf16[1,8,16,768]{3,2,1,0:T(8,128)(2,1)S(1)}, bf16[4,32,768]{2,1,0:T(8,128)(2,1)S(1)}, bf16[4,32,15...) custom-call(bf16[4,3072]{1,0:T(4,128)(2,1)} %tokens_ref.3, bf16[4,3072]{1,0:T(4,128)(2,1)} %cot_ref.3, ...), custom_call_target="tpu_custom_call" | custom-call | flops 1207959552 | bytes 18874368 | tf_op jit(solution)/shard_map/pallas_call | solution.py:301
  31.1 0.0 copy-done.1
  31.1 0.0 copy-done
  31.1 3.0 %shard_map.76 = (bf16[4,3072]{1,0:T(4,128)(2,1)}, bf16[4,3072]{1,0:T(4,128)(2,1)}, bf16[768,1536]{1,0:T(8,128)(2,1)}, bf16[1536,768]{1,0:T(8,128)(2,1)}) custom-call(bf16[4,3072]{1,0:T(4,128)(2,1)S(1)} %copy-done, bf16[4,3072]{1,0:T(4,128)(2,1)S(1)} %copy-done.1, bf16[1,8,16,768]{3,2,1,0:T(8,128)(2,1)S(1)} %get-tuple-element.9.rs_out, ...), custom_call_target="tpu_custom_call" | custom-call | flops 301989888 | bytes 4718592 | tf_op jit(solution)/shard_map/pallas_call | solution.py:335
Async XLA Ops:
  0.6 30.4 %copy-start.1 = (bf16[4,3072]{1,0:T(4,128)(2,1)S(1)}, bf16[4,3072]{1,0:T(4,128)(2,1)}, u32[]{:S(2)}) copy-start(bf16[4,3072]{1,0:T(4,128)(2,1)} %cot_ref.3) | copy-start | bytes 73732
  0.6 30.4 %copy-start = (bf16[4,3072]{1,0:T(4,128)(2,1)S(1)}, bf16[4,3072]{1,0:T(4,128)(2,1)}, u32[]{:S(2)}) copy-start(bf16[4,3072]{1,0:T(4,128)(2,1)} %tokens_ref.3) | copy-start | bytes 73732

commit v7 on v6

--- a/solution.py
+++ b/solution.py
@@ -10,7 +10,7 @@
 ROOT_HALF = 0.7071067811865476
 DENSITY_SCALE = 0.3989422804014327
 TILE_ROWS = 16
-HALVES = 1
+HALVES = 2
 MESH = pl.DeviceIdType.MESH
 F32 = jnp.float32
 BF16 = jnp.bfloat16

time: 34.3 us -> 35 us (1.020)
  Pallas kernels: 33.4 us -> 34.2 us
    pallas_call x1, Pallas kernels: 30.4 us -> 31 us  [body(): pl.pallas_call(functools.partial(exchange_kernel, n_dp, n_mp), out_shape=...]
where the time goes in v7:
time: 35 us; the launch traced here: 34.9 us
  Pallas kernels  34.2 us (98%)
  between operations  0.67 us (2%)
    pallas_call x1, Pallas kernels, body(): pl.pallas_call(functools.partial(exchange_kernel, n_dp, n_mp), out_shape=...  31 us
    pallas_call x1, Pallas kernels, body(): pl.pallas_call(result_kernel, out_shape=(jax.ShapeDtypeStruct(tokens.shap...  3.2 us

profile of v7, /device:TPU:0, one launch (start us, length us, event | category | flops | bytes accessed | tf_op | source)
XLA Modules:
  0.0 34.9 jit_solution(4104604158919390590)
XLA Ops:
  0.6 0.0 copy-start.1
  0.6 0.0 copy-start
  0.7 31.0 %shard_map.75 = (bf16[2,8,16,384]{3,2,1,0:T(8,128)(2,1)S(1)}, bf16[2,8,16,384]{3,2,1,0:T(8,128)(2,1)S(1)}, bf16[4,32,768]{2,1,0:T(8,128)(2,1)S(1)}, bf16[4,32,15...) custom-call(bf16[4,3072]{1,0:T(4,128)(2,1)} %tokens_ref.3, bf16[4,3072]{1,0:T(4,128)(2,1)} %cot_ref.3, ...), custom_call_target="tpu_custom_call" | custom-call | flops 1207959552 | bytes 18874368 | tf_op jit(solution)/shard_map/pallas_call | solution.py:301
  31.6 0.0 copy-done.1
  31.6 0.0 copy-done
  31.7 3.2 %shard_map.76 = (bf16[4,3072]{1,0:T(4,128)(2,1)}, bf16[4,3072]{1,0:T(4,128)(2,1)}, bf16[768,1536]{1,0:T(8,128)(2,1)}, bf16[1536,768]{1,0:T(8,128)(2,1)}) custom-call(bf16[4,3072]{1,0:T(4,128)(2,1)S(1)} %copy-done, bf16[4,3072]{1,0:T(4,128)(2,1)S(1)} %copy-done.1, bf16[2,8,16,384]{3,2,1,0:T(8,128)(2,1)S(1)} %get-tuple-element.9.rs_out, ...), custom_call_target="tpu_custom_call" | custom-call | flops 301989888 | bytes 4718592 | tf_op jit(solution)/shard_map/pallas_call | solution.py:335
Async XLA Ops:
  0.6 31.0 %copy-start.1 = (bf16[4,3072]{1,0:T(4,128)(2,1)S(1)}, bf16[4,3072]{1,0:T(4,128)(2,1)}, u32[]{:S(2)}) copy-start(bf16[4,3072]{1,0:T(4,128)(2,1)} %cot_ref.3) | copy-start | bytes 73732
  0.6 31.0 %copy-start = (bf16[4,3072]{1,0:T(4,128)(2,1)S(1)}, bf16[4,3072]{1,0:T(4,128)(2,1)}, u32[]{:S(2)}) copy-start(bf16[4,3072]{1,0:T(4,128)(2,1)} %tokens_ref.3) | copy-start | bytes 73732
